TPU v7x, 32 devices: a whole 2x2x4 slice. The times are simulated.
32 devices in a mesh: dp: 4 (over y, core), seq: 8 (over z, x).
Axes of the slice: x: 2, y: 2, z: 4, core: 2. Of those that a mesh axis runs over, the one named last changes fastest.
Arguments:
- tokens: bfloat16 [4096, 1024], P(('dp', 'seq')), may hold values from -6 to 6
- span_order: int32 [4, 16], P('dp'), may hold values from 0 to 15, each once within a row
- w_query: bfloat16 [1024, 2048], P(('dp', 'seq')), may hold values from -0.1875 to 0.1875
- key_matrix: bfloat16 [1024, 1024], P(('dp', 'seq')), may hold values from -0.1875 to 0.1875
- value_matrix: bfloat16 [1024, 1024], P(('dp', 'seq')), may hold values from -0.1875 to 0.1875
- w_output: bfloat16 [2048, 1024], P(None, ('dp', 'seq')), may hold values from -2 to 2
- w_gate: bfloat16 [1024, 3072], P(('dp', 'seq')), may hold values from -0.1875 to 0.1875
- w_up: bfloat16 [1024, 3072], P(('dp', 'seq')), may hold values from -0.1875 to 0.1875
- w_down: bfloat16 [3072, 1024], P(None, ('dp', 'seq')), may hold values from -0.109375 to 0.109375
- norm_gains: bfloat16 [2, 1024], P(None, ('dp', 'seq')), may hold values from 0.5 to 1.5
- head_gains: bfloat16 [2, 128], replicated, may hold values from 0.5 to 1.5
- cotangent: bfloat16 [4096, 1024], P(('dp', 'seq')), may hold values from -6 to 6
Outputs:
- output: bfloat16 [4096, 1024], P(('dp', 'seq'))
- grad_input: bfloat16 [4096, 1024], P(('dp', 'seq'))
- grad_w_query: float32 [1024, 2048], P(('dp', 'seq'))
- grad_w_key: float32 [1024, 1024], P(('dp', 'seq'))
- grad_w_value: float32 [1024, 1024], P(('dp', 'seq'))
- grad_w_output: float32 [2048, 1024], P(None, ('dp', 'seq'))
- grad_w_gate: float32 [1024, 3072], P(('dp', 'seq'))
- grad_w_up: float32 [1024, 3072], P(('dp', 'seq'))
- grad_w_down: float32 [3072, 1024], P(None, ('dp', 'seq'))
- grad_norm_gains: float32 [2, 1024], P(None, ('dp', 'seq'))
- grad_head_gains: float32 [2, 128], replicated
Inputs may be any that keep to these rules, and one draw needn't show every extreme that they name: Each row is a permutation of the 16 spans of its sequence; slot k holds the 64 tokens at positions span_order[s, k] * 64 onwards, and device j of seq holds slots 2 j and 2 j + 1.
All inputs are finite; a program needn't handle non-finite values.
Results may differ from a plain program's by a relative error of at most 0.02.
Values may be sent and summed in bfloat16 or wider, within the bound.
No kernel may reach another device: no remote copies, remote signals or barrier semaphores. Data moves between devices by JAX's collectives and lax.ppermute only.
A program may use at most 320 MiB of HBM per device.

v0:
```python
import math

import jax
import jax.numpy as jnp
from jax import lax
from jax.sharding import PartitionSpec as P

eps_model = 1e-06
rope_base = 1000000.0
masked_value = -1e30


def passed_along(array, axis, by):
    length = lax.axis_size(axis)
    return lax.ppermute(array, axis, [(i, (i + by) % length) for i in range(length)])


def rms_scale(values, gain):
    inverse = lax.rsqrt(jnp.mean(values * values, axis=-1, keepdims=True) + eps_model)
    return values * inverse * gain


def rope_tables(positions, head_dim):
    half_dim = head_dim // 2
    freqs = rope_base ** (-(jnp.arange(half_dim, dtype=jnp.float32) * 2.0) / head_dim)
    angles = positions.astype(jnp.float32)[:, None] * freqs[None, :]
    cosine = jnp.cos(angles)
    sine = jnp.sin(angles)
    return (jnp.concatenate([cosine, cosine], -1), jnp.concatenate([sine, sine], -1))


def rotate(values, cosine, sine):
    half_dim = values.shape[-1] // 2
    turned = jnp.concatenate([-values[..., half_dim:], values[..., :half_dim]], -1)
    return values * cosine[:, None, :] + turned * sine[:, None, :]


def head_prep(flat, gain, cosine, sine):
    row_count = flat.shape[0]
    shaped = flat.reshape(row_count, -1, gain.shape[0])
    return rotate(rms_scale(shaped, gain), cosine, sine).reshape(row_count, -1)


def span_positions(order_row, start, count, span_len):
    row_index = start + jnp.arange(count, dtype=jnp.int32)
    slot_index = row_index // span_len
    table = (
        slot_index[:, None] == jnp.arange(order_row.shape[0], dtype=jnp.int32)[None, :]
    ).astype(jnp.int32)
    return jnp.sum(table * order_row[None, :], axis=1) * span_len + row_index % span_len


def block_size(count):
    return count if count <= 512 else math.gcd(count, 512)


def contract_rows(left, right):
    return lax.dot_general(
        left, right, (((0,), (0,)), ((), ())), preferred_element_type=jnp.float32
    )


def contract_cols(left, right):
    return lax.dot_general(
        left, right, (((1,), (1,)), ((), ())), preferred_element_type=jnp.float32
    )


def forward_block(state, query_heads, query_pos, key_block, value_block, key_pos, head_dim):
    run_max, run_total, accum = state
    kv_heads = key_block.shape[1] // head_dim
    key_heads = key_block.reshape(-1, kv_heads, head_dim)
    value_heads = value_block.reshape(-1, kv_heads, head_dim)
    scores = jnp.einsum(
        "tkgd,skd->kgts", query_heads, key_heads, preferred_element_type=jnp.float32
    ) * head_dim ** (-0.5)
    allowed = key_pos[None, :] <= query_pos[:, None]
    scores = jnp.where(allowed, scores, masked_value)
    new_max = jnp.maximum(run_max, jnp.max(scores, axis=-1))
    probs = jnp.where(allowed, jnp.exp(scores - new_max[..., None]), 0.0)
    factor = jnp.exp(run_max - new_max)
    new_total = run_total * factor + jnp.sum(probs, axis=-1)
    accum = accum * factor[..., None] + jnp.einsum(
        "kgts,skd->kgtd",
        probs.astype(jnp.bfloat16),
        value_heads,
        preferred_element_type=jnp.float32,
    )
    return (new_max, new_total, accum)


def backward_block(
    query_heads, grad_heads, log_total, delta, query_pos, key_block, value_block, key_pos, head_dim
):
    kv_heads = key_block.shape[1] // head_dim
    key_heads = key_block.reshape(-1, kv_heads, head_dim)
    value_heads = value_block.reshape(-1, kv_heads, head_dim)
    scale = head_dim ** (-0.5)
    scores = (
        jnp.einsum("tkgd,skd->kgts", query_heads, key_heads, preferred_element_type=jnp.float32)
        * scale
    )
    allowed = key_pos[None, :] <= query_pos[:, None]
    probs = jnp.where(allowed, jnp.exp(scores - log_total[..., None]), 0.0)
    grad_value = jnp.einsum(
        "kgts,tkgd->skd", probs.astype(jnp.bfloat16), grad_heads, preferred_element_type=jnp.float32
    )
    grad_probs = jnp.einsum(
        "tkgd,skd->kgts", grad_heads, value_heads, preferred_element_type=jnp.float32
    )
    grad_scores = (probs * (grad_probs - delta[..., None])).astype(jnp.bfloat16)
    grad_query = (
        jnp.einsum("kgts,skd->tkgd", grad_scores, key_heads, preferred_element_type=jnp.float32)
        * scale
    )
    grad_key = (
        jnp.einsum("kgts,tkgd->skd", grad_scores, query_heads, preferred_element_type=jnp.float32)
        * scale
    )
    count = key_block.shape[0]
    return (
        grad_query,
        jnp.concatenate([grad_key.reshape(count, -1), grad_value.reshape(count, -1)], 1),
    )


def swiglu(gate, up_proj):
    return jax.nn.silu(gate) * up_proj


def shards(
    tokens,
    span_order,
    w_query,
    key_matrix,
    value_matrix,
    w_output,
    w_gate,
    w_up,
    w_down,
    norm_gains,
    head_gains,
    cotangent,
):
    row_count = tokens.shape[0]
    span_len = row_count // 2
    head_dim = head_gains.shape[1]
    kv_heads = key_matrix.shape[1] // head_dim
    groups = w_query.shape[1] // key_matrix.shape[1]
    order_row = span_order[0]
    seq_devices = lax.axis_size("seq")
    seq_index = lax.axis_index("seq")
    own_start = seq_index * row_count

    def positions_of(start, count):
        return span_positions(order_row, start, count, span_len)

    query_pos = positions_of(own_start, row_count)
    cosine, sine = rope_tables(query_pos, head_dim)
    gains_head = head_gains.astype(jnp.float32)

    def prepare(flat, gain):
        return head_prep(flat, gain, cosine, sine)

    wq_full, wk_full, wv_full, wo_full, gains_full = (
        lax.all_gather(w_query, ("dp", "seq"), axis=0, tiled=True),
        lax.all_gather(key_matrix, ("dp", "seq"), axis=0, tiled=True),
        lax.all_gather(value_matrix, ("dp", "seq"), axis=0, tiled=True),
        lax.all_gather(w_output, ("dp", "seq"), axis=1, tiled=True),
        lax.all_gather(norm_gains, ("dp", "seq"), axis=1, tiled=True),
    )
    gains_full = gains_full.astype(jnp.float32)
    inputs = tokens.astype(jnp.float32)
    normed, norm_back = jax.vjp(rms_scale, inputs, gains_full[0])
    normed_low = normed.astype(jnp.bfloat16)
    query_pre = jnp.dot(normed_low, wq_full, preferred_element_type=jnp.float32)
    key_pre = jnp.dot(normed_low, wk_full, preferred_element_type=jnp.float32)
    value_low = jnp.dot(normed_low, wv_full, preferred_element_type=jnp.float32).astype(
        jnp.bfloat16
    )
    query_rot, query_back = jax.vjp(prepare, query_pre, gains_head[0])
    key_rot, key_back = jax.vjp(prepare, key_pre, gains_head[1])
    query_heads = query_rot.astype(jnp.bfloat16).reshape(row_count, kv_heads, groups, head_dim)
    key_low = key_rot.astype(jnp.bfloat16)
    latest = jnp.max(query_pos)
    start_state = (
        jnp.full((kv_heads, groups, row_count), masked_value, jnp.float32),
        jnp.zeros((kv_heads, groups, row_count), jnp.float32),
        jnp.zeros((kv_heads, groups, row_count, head_dim), jnp.float32),
    )
    state = start_state
    key_piece = lax.all_gather(key_low, "seq", axis=0, tiled=True)
    value_piece = lax.all_gather(value_low, "seq", axis=0, tiled=True)
    count = key_piece.shape[0]
    size = block_size(count)
    number = count // size
    key_blocks = key_piece.reshape(number, size, key_piece.shape[1])
    value_blocks = value_piece.reshape(number, size, value_piece.shape[1])

    def attend_one_block(carried, item):
        index, key_block, value_block = item
        key_pos = positions_of(index * size, size)

        def attend_compute(inner):
            return forward_block(
                inner, query_heads, query_pos, key_block, value_block, key_pos, head_dim
            )

        def attend_unchanged(inner):
            return inner

        return (
            lax.cond(jnp.min(key_pos) <= latest, attend_compute, attend_unchanged, carried),
            None,
        )

    state, _ = lax.scan(
        attend_one_block, state, (jnp.arange(number, dtype=jnp.int32), key_blocks, value_blocks)
    )
    final_max, final_total, accum = state
    attended_heads = (accum / final_total[..., None]).transpose(2, 0, 1, 3)
    attention_output = attended_heads.reshape(row_count, -1)
    log_total = final_max + jnp.log(final_total)
    attended_low = attention_output.astype(jnp.bfloat16)
    middle = inputs + jnp.dot(attended_low, wo_full, preferred_element_type=jnp.float32)
    wg_full, wu_full, wd_full = (
        lax.all_gather(w_gate, ("dp", "seq"), axis=0, tiled=True),
        lax.all_gather(w_up, ("dp", "seq"), axis=0, tiled=True),
        lax.all_gather(w_down, ("dp", "seq"), axis=1, tiled=True),
    )
    normed_two, norm_two_back = jax.vjp(rms_scale, middle, gains_full[1])
    normed_two_low = normed_two.astype(jnp.bfloat16)
    gate = jnp.dot(normed_two_low, wg_full, preferred_element_type=jnp.float32)
    up_proj = jnp.dot(normed_two_low, wu_full, preferred_element_type=jnp.float32)
    hidden, swiglu_back = jax.vjp(swiglu, gate, up_proj)
    hidden_low = hidden.astype(jnp.bfloat16)
    output = middle + jnp.dot(hidden_low, wd_full, preferred_element_type=jnp.float32)
    grad_out = cotangent.astype(jnp.float32)
    wg_full, wu_full, wd_full = (
        lax.all_gather(w_gate, ("dp", "seq"), axis=0, tiled=True),
        lax.all_gather(w_up, ("dp", "seq"), axis=0, tiled=True),
        lax.all_gather(w_down, ("dp", "seq"), axis=1, tiled=True),
    )
    grad_down_turned = contract_rows(cotangent, hidden_low)
    grad_hidden = contract_cols(cotangent, wd_full)
    grad_gate, grad_up = swiglu_back(grad_hidden)
    gate_low = grad_gate.astype(jnp.bfloat16)
    up_low = grad_up.astype(jnp.bfloat16)
    grad_wg = contract_rows(normed_two_low, gate_low)
    grad_wu = contract_rows(normed_two_low, up_low)
    grad_normed_two = contract_cols(gate_low, wg_full) + contract_cols(up_low, wu_full)
    grad_middle_norm, grad_gain_two = norm_two_back(grad_normed_two)
    feed_grads = (
        lax.psum_scatter(grad_wg, ("dp", "seq"), scatter_dimension=0, tiled=True),
        lax.psum_scatter(grad_wu, ("dp", "seq"), scatter_dimension=0, tiled=True),
        lax.psum_scatter(grad_down_turned, ("dp", "seq"), scatter_dimension=0, tiled=True),
    )
    grad_middle = grad_out + grad_middle_norm
    wq_full, wk_full, wv_full, wo_full = (
        lax.all_gather(w_query, ("dp", "seq"), axis=0, tiled=True),
        lax.all_gather(key_matrix, ("dp", "seq"), axis=0, tiled=True),
        lax.all_gather(value_matrix, ("dp", "seq"), axis=0, tiled=True),
        lax.all_gather(w_output, ("dp", "seq"), axis=1, tiled=True),
    )
    middle_low = grad_middle.astype(jnp.bfloat16)
    grad_wo_turned = contract_rows(middle_low, attended_low)
    attention_output_gradient = contract_cols(middle_low, wo_full).astype(jnp.bfloat16)
    grad_heads = attention_output_gradient.reshape(row_count, kv_heads, groups, head_dim)
    delta = jnp.sum(grad_heads.astype(jnp.float32) * attended_heads, axis=-1).transpose(1, 2, 0)

    def piece_back(grad_query_all, key_piece, value_piece, start):
        count = key_piece.shape[0]
        size = block_size(count)
        number = count // size
        key_blocks = key_piece.reshape(number, size, key_piece.shape[1])
        value_blocks = value_piece.reshape(number, size, value_piece.shape[1])

        def piece_one_block(grad_query_run, item):
            index, key_block, value_block = item
            key_pos = positions_of(start + index * size, size)

            def piece_compute(inner):
                grad_query, grad_kv = backward_block(
                    query_heads,
                    grad_heads,
                    log_total,
                    delta,
                    query_pos,
                    key_block,
                    value_block,
                    key_pos,
                    head_dim,
                )
                return (inner + grad_query, grad_kv)

            def piece_unchanged(inner):
                return (inner, jnp.zeros((size, 2 * kv_heads * head_dim), jnp.float32))

            return lax.cond(
                jnp.min(key_pos) <= latest, piece_compute, piece_unchanged, grad_query_run
            )

        grad_query_all, stacked = lax.scan(
            piece_one_block,
            grad_query_all,
            (jnp.arange(number, dtype=jnp.int32), key_blocks, value_blocks),
        )
        return (grad_query_all, stacked.reshape(count, -1))

    start_query = jnp.zeros((row_count, kv_heads, groups, head_dim), jnp.float32)

    def cycle_step(step, carried):
        grad_query_all, key_piece, value_piece, partial_value = carried
        source = (seq_index - step + seq_devices) % seq_devices
        grad_query_all, local_kv = piece_back(
            grad_query_all, key_piece, value_piece, source * row_count
        )
        partial_value = partial_value + local_kv
        key_piece, value_piece = passed_along((key_piece, value_piece), "seq", 1)
        partial_value = passed_along(partial_value.astype(jnp.bfloat16), "seq", 1).astype(
            partial_value.dtype
        )
        return (grad_query_all, key_piece, value_piece, partial_value)

    initial_cycle_step = (
        start_query,
        key_low,
        value_low,
        jnp.zeros((row_count, 2 * kv_heads * head_dim), jnp.float32),
    )
    grad_query_rot, _, _, grad_kv = lax.fori_loop(0, seq_devices, cycle_step, initial_cycle_step)
    split_at = kv_heads * head_dim
    grad_query_pre, grad_gain_query = query_back(grad_query_rot.reshape(row_count, -1))
    grad_key_pre, grad_gain_key = key_back(grad_kv[:, :split_at])
    query_grad_low = grad_query_pre.astype(jnp.bfloat16)
    key_grad_low = grad_key_pre.astype(jnp.bfloat16)
    value_grad_low = grad_kv[:, split_at:].astype(jnp.bfloat16)
    grad_wq = contract_rows(normed_low, query_grad_low)
    grad_wk = contract_rows(normed_low, key_grad_low)
    grad_wv = contract_rows(normed_low, value_grad_low)
    grad_normed = (
        contract_cols(query_grad_low, wq_full)
        + contract_cols(key_grad_low, wk_full)
        + contract_cols(value_grad_low, wv_full)
    )
    grad_input_norm, grad_gain_one = norm_back(grad_normed)
    grad_input = grad_middle + grad_input_norm
    gains_turned = jnp.stack([grad_gain_one, grad_gain_two], axis=1)
    attention_grads = (
        lax.psum_scatter(grad_wq, ("dp", "seq"), scatter_dimension=0, tiled=True),
        lax.psum_scatter(grad_wk, ("dp", "seq"), scatter_dimension=0, tiled=True),
        lax.psum_scatter(grad_wv, ("dp", "seq"), scatter_dimension=0, tiled=True),
        lax.psum_scatter(grad_wo_turned, ("dp", "seq"), scatter_dimension=0, tiled=True),
        lax.psum_scatter(gains_turned, ("dp", "seq"), scatter_dimension=0, tiled=True),
    )
    head_grads = lax.psum(jnp.stack([grad_gain_query, grad_gain_key]), ("dp", "seq"))
    return (
        output.astype(jnp.bfloat16),
        grad_input.astype(jnp.bfloat16),
        attention_grads[0],
        attention_grads[1],
        attention_grads[2],
        attention_grads[3].T,
        feed_grads[0],
        feed_grads[1],
        feed_grads[2].T,
        attention_grads[4].T,
        head_grads,
    )


def solution(mesh):
    return jax.shard_map(
        shards,
        mesh=mesh,
        in_specs=(
            P(("dp", "seq"), None),
            P("dp", None),
            P(("dp", "seq"), None),
            P(("dp", "seq"), None),
            P(("dp", "seq"), None),
            P(None, ("dp", "seq")),
            P(("dp", "seq"), None),
            P(("dp", "seq"), None),
            P(None, ("dp", "seq")),
            P(None, ("dp", "seq")),
            P(),
            P(("dp", "seq"), None),
        ),
        out_specs=(
            P(("dp", "seq"), None),
            P(("dp", "seq"), None),
            P(("dp", "seq"), None),
            P(("dp", "seq"), None),
            P(("dp", "seq"), None),
            P(None, ("dp", "seq")),
            P(("dp", "seq"), None),
            P(("dp", "seq"), None),
            P(None, ("dp", "seq")),
            P(None, ("dp", "seq")),
            P(),
        ),
        check_vma=False,
    )
```

profile of v0, /device:TPU:0, one launch (start us, length us, event | category | flops | bytes accessed | tf_op | source)
XLA Modules:
  0.0 2192.5 jit_solution(14153159320302625263)
XLA Ops:
  8.7 69.5 %all-gather = bf16[32,32,2]{1,2,0:T(2,128)(2,1)S(1)} all-gather(bf16[1,32,2]{1,2,0:T(2,128)(2,1)} %bitcast.281), channel_id=1, replica_groups=mesh['dp'=4,'seq'=8] {'dp','seq'}, dimensions={0}, use_global_device_ids=true | all-gather | bytes 4224 | tf_op jit(solution)/shard_map/all_gather | solution.py:170
  86.6 42.1 %all-gather.17.cloned.1.call-done = bf16[1024,1024]{1,0:T(8,128)(2,1)} async-done(((bf16[32,1024]{1,0:T(8,128)(2,1)}), bf16[1024,1024]{1,0:T(8,128)(2,1)}) %all-gather.17.cloned.1.call-update) | async-done | bytes 2097168 | tf_op jit(solution)/shard_map/all_gather | solution.py:168
  136.7 42.3 %all-gather.13.cloned.1.call-done = bf16[1024,1024]{1,0:T(8,128)(2,1)} async-done(((bf16[128,1024]{1,0:T(8,128)(2,1)}), bf16[1024,1024]{1,0:T(8,128)(2,1)}) %all-gather.13.cloned.1.call-update) | async-done | bytes 2097168 | tf_op jit(solution)/shard_map/all_gather | solution.py:192
  181.9 46.9 %all-gather.19.cloned.1.call-done = bf16[1024,1024]{1,0:T(8,128)(2,1)} async-done(((bf16[128,1024]{1,0:T(8,128)(2,1)}), bf16[1024,1024]{1,0:T(8,128)(2,1)}) %all-gather.19.cloned.1.call-update) | async-done | bytes 2097168 | tf_op jit(solution)/shard_map/all_gather | solution.py:193
  232.8 59.5 %all-gather.15.cloned.1.call-done = bf16[1024,2048]{1,0:T(8,128)(2,1)} async-done(((bf16[32,2048]{1,0:T(8,128)(2,1)}), bf16[1024,2048]{1,0:T(8,128)(2,1)}) %all-gather.15.cloned.1.call-update) | async-done | bytes 4194320 | tf_op jit(solution)/shard_map/all_gather | solution.py:166
  304.8 21.8 while.53
  328.4 27.5 %all-gather.21.cloned.1.call-done = bf16[2048,1024]{0,1:T(8,128)(2,1)} async-done(((bf16[2048,32]{0,1:T(8,128)(2,1)}), bf16[2048,1024]{0,1:T(8,128)(2,1)}) %all-gather.21.cloned.1.call-update) | async-done | bytes 4194320 | tf_op jit(solution)/shard_map/all_gather | solution.py:169
  360.5 66.4 %all-gather.23.cloned.1.call-done = bf16[1024,3072]{1,0:T(8,128)(2,1)} async-done(((bf16[32,3072]{1,0:T(8,128)(2,1)}), bf16[1024,3072]{1,0:T(8,128)(2,1)}) %all-gather.23.cloned.1.call-update) | async-done | bytes 6291472 | tf_op jit(solution)/shard_map/all_gather | solution.py:227
  431.9 66.1 %all-gather.25.cloned.1.call-done = bf16[1024,3072]{1,0:T(8,128)(2,1)} async-done(((bf16[32,3072]{1,0:T(8,128)(2,1)}), bf16[1024,3072]{1,0:T(8,128)(2,1)}) %all-gather.25.cloned.1.call-update) | async-done | bytes 6291472 | tf_op jit(solution)/shard_map/all_gather | solution.py:228
  502.8 66.1 %all-gather.27.cloned.1.call-done = bf16[3072,1024]{0,1:T(8,128)(2,1)} async-done(((bf16[3072,32]{0,1:T(8,128)(2,1)}), bf16[3072,1024]{0,1:T(8,128)(2,1)}) %all-gather.27.cloned.1.call-update) | async-done | bytes 6291472 | tf_op jit(solution)/shard_map/all_gather | solution.py:229
  586.0 271.8 %while.54 = (s32[]{:T(128)}, f32[128,8,2,128]{3,0,2,1:T(8,128)S(1)}, bf16[128,1024]{1,0:T(8,128)(2,1)}, bf16[128,1024]{1,0:T(8,128)(2,1)}, f32[128,2048]{0,1:T(8...) while((s32[]{:T(128)}, ...), condition=%wide.region_21.22_spmd.clone, body=%wide.region_16.21_spmd.clone.sunk | while | flops 339371776 | bytes 25481348 | solution.py:331
  599.9 13.3 collective-permute-done.2
  636.1 16.1 collective-permute-done.2
  671.8 14.3 collective-permute-done.2
  839.3 12.7 collective-permute-done.2
  936.1 63.0 %psum.7 = f32[2,128]{1,0:T(2,128)} all-reduce(f32[2,128]{1,0:T(2,128)S(1)} %pad_maximum_fusion.4), channel_id=1, replica_groups=mesh['dp'=4,'seq'=8] {'dp','seq'}, use_global_device_ids=true, to_apply=%region_37.38 | all-reduce | flops 256 | bytes 2048 | tf_op jit(solution)/shard_map/psum | solution.py:356
  1005.7 36.3 %reduce-scatter.27.cloned.1.call-done = f32[32,2]{1,0:T(8,128)} async-done(((f32[1024,2]{1,0:T(8,128)}), f32[32,2]{1,0:T(8,128)}) %reduce-scatter.27.cloned.1.call-update) | async-done | bytes 272
  1043.4 141.7 %reduce-scatter.15.cloned.1.call-done = f32[32,1024]{1,0:T(8,128)} async-done(((f32[1024,1024]{1,0:T(8,128)}), f32[32,1024]{1,0:T(8,128)}) %reduce-scatter.15.cloned.1.call-update) | async-done | bytes 131088 | tf_op jit(solution)/shard_map/reduce_scatter | solution.py:351
  1185.1 142.9 %reduce-scatter.17.cloned.1.call-done = f32[32,1024]{1,0:T(8,128)} async-done(((f32[1024,1024]{1,0:T(8,128)}), f32[32,1024]{1,0:T(8,128)}) %reduce-scatter.17.cloned.1.call-update) | async-done | bytes 131088 | tf_op jit(solution)/shard_map/reduce_scatter | solution.py:352
  1328.0 160.3 %reduce-scatter.21.cloned.1.call-done = f32[32,3072]{1,0:T(8,128)} async-done(((f32[1024,3072]{1,0:T(8,128)}), f32[32,3072]{1,0:T(8,128)}) %reduce-scatter.21.cloned.1.call-update) | async-done | bytes 393232 | tf_op jit(solution)/shard_map/reduce_scatter | solution.py:254
  1488.3 161.3 %reduce-scatter.23.cloned.1.call-done = f32[32,3072]{1,0:T(8,128)} async-done(((f32[1024,3072]{1,0:T(8,128)}), f32[32,3072]{1,0:T(8,128)}) %reduce-scatter.23.cloned.1.call-update) | async-done | bytes 393232 | tf_op jit(solution)/shard_map/reduce_scatter | solution.py:255
  1649.5 185.9 %reduce-scatter.19.cloned.1.call-done = f32[32,2048]{1,0:T(8,128)} async-done(((f32[1024,2048]{1,0:T(8,128)}), f32[32,2048]{1,0:T(8,128)}) %reduce-scatter.19.cloned.1.call-update) | async-done | bytes 262160 | tf_op jit(solution)/shard_map/reduce_scatter | solution.py:353
  1835.4 187.8 %reduce-scatter.13.cloned.1.call-done = f32[32,2048]{1,0:T(8,128)} async-done(((f32[1024,2048]{1,0:T(8,128)}), f32[32,2048]{1,0:T(8,128)}) %reduce-scatter.13.cloned.1.call-update) | async-done | bytes 262160 | tf_op jit(solution)/shard_map/reduce_scatter | solution.py:350
  2023.2 162.5 %reduce-scatter.25.cloned.1.call-done = f32[32,3072]{1,0:T(8,128)} async-done(((f32[1024,3072]{1,0:T(8,128)}), f32[32,3072]{1,0:T(8,128)}) %reduce-scatter.25.cloned.1.call-update) | async-done | bytes 393232
  (473 shorter events, 421.1 us)
Async XLA Ops:
  7.2 74.2 %all-gather.11.cloned.1.call-start = ((), (), s32[]{:S(2)}) async-start(), calls=%async_computation.8 | async-start | bytes 2162688 | tf_op jit(solution)/shard_map/all_gather | solution.py:167
  7.9 120.8 %all-gather.17.cloned.1.call-start = ((), (), s32[]{:S(2)}) async-start(), calls=%async_computation.11 | async-start | bytes 2162688 | tf_op jit(solution)/shard_map/all_gather | solution.py:168
  8.7 170.4 %all-gather.13.cloned.1.call-start = ((), (), s32[]{:S(2)}) async-start(), calls=%async_computation.9 | async-start | bytes 2359296 | tf_op jit(solution)/shard_map/all_gather | solution.py:192
  86.6 142.3 %all-gather.19.cloned.1.call-start = ((), (), s32[]{:S(2)}) async-start(), calls=%async_computation.12 | async-start | bytes 2359296 | tf_op jit(solution)/shard_map/all_gather | solution.py:193
  131.5 160.8 %all-gather.15.cloned.1.call-start = ((), (), s32[]{:S(2)}) async-start(), calls=%async_computation.10 | async-start | bytes 4325376 | tf_op jit(solution)/shard_map/all_gather | solution.py:166
  132.1 223.8 %all-gather.21.cloned.1.call-start = ((), (), s32[]{:S(2)}) async-start(), calls=%async_computation.13 | async-start | bytes 4325376 | tf_op jit(solution)/shard_map/all_gather | solution.py:169
  132.7 294.2 %all-gather.23.cloned.1.call-start = ((), (), s32[]{:S(2)}) async-start(), calls=%async_computation.14 | async-start | bytes 6488064 | tf_op jit(solution)/shard_map/all_gather | solution.py:227
  133.4 364.5 %all-gather.25.cloned.1.call-start = ((), (), s32[]{:S(2)}) async-start(), calls=%async_computation.15 | async-start | bytes 6488064 | tf_op jit(solution)/shard_map/all_gather | solution.py:228
  134.2 434.8 %all-gather.27.cloned.1.call-start = ((), (), s32[]{:S(2)}) async-start(), calls=%async_computation.16 | async-start | bytes 6488064 | tf_op jit(solution)/shard_map/all_gather | solution.py:229
  134.9 907.2 %reduce-scatter.27.cloned.1.call-start = ((), (), s32[]{:S(2)}) async-start(), calls=%async_computation.24 | async-start | bytes 540672
  596.9 22.0 %collective-permute-start = (bf16[128,1024]{1,0:T(8,128)(2,1)S(1)}, bf16[128,1024]{1,0:T(8,128)(2,1)}, u32[]{:S(2)}, u32[]{:S(2)}) collective-permute-start(bf16[128,1024]{1,0:T(8,128)(2,1)S(1)} %copy.277), channel_id=1, source_target_pairs={{0,1},{1,2},{2,3},{3,4},{4,5},{5,6},{6,7},{7,0},{8,9},{9,10},{10,1... | collective-permute-start | bytes 786440 | tf_op jit(solution)/shard_map/while/body/eval_jaxpr/ppermute | solution.py:15
  598.5 25.4 %collective-permute-start.1 = (bf16[128,1024]{1,0:T(8,128)(2,1)S(1)}, bf16[128,1024]{1,0:T(8,128)(2,1)}, u32[]{:S(2)}, u32[]{:S(2)}) collective-permute-start(bf16[128,1024]{1,0:T(8,128)(2,1)S(1)} %copy.278), channel_id=1, source_target_pairs={{0,1},{1,2},{2,3},{3,4},{4,5},{5,6},{6,7},{7,0},{8,9},{9,10},{10,1... | collective-permute-start | bytes 786440 | tf_op jit(solution)/shard_map/while/body/eval_jaxpr/ppermute | solution.py:15
  634.4 21.1 collective-permute-start
  635.5 22.7 %collective-permute-start.1 = (bf16[128,1024]{1,0:T(8,128)(2,1)S(1)}, bf16[128,1024]{1,0:T(8,128)(2,1)}, u32[]{:S(2)}, u32[]{:S(2)}) collective-permute-start(bf16[128,1024]{1,0:T(8,128)(2,1)S(1)} %copy.278), channel_id=1, source_target_pairs={{0,1},{1,2},{2,3},{3,4},{4,5},{5,6},{6,7},{7,0},{8,9},{9,10},{10,1... | collective-permute-start | bytes 786440 | tf_op jit(solution)/shard_map/while/body/eval_jaxpr/ppermute | solution.py:15
  668.8 20.3 collective-permute-start
  671.8 20.1 collective-permute-start.1
  835.9 19.1 collective-permute-start
  883.8 301.3 %reduce-scatter.15.cloned.1.call-start = ((), (), s32[]{:S(2)}) async-start(), calls=%async_computation.18 | async-start | bytes 4325376 | tf_op jit(solution)/shard_map/reduce_scatter | solution.py:351
  886.7 441.3 %reduce-scatter.17.cloned.1.call-start = ((), (), s32[]{:S(2)}) async-start(), calls=%async_computation.19 | async-start | bytes 4325376 | tf_op jit(solution)/shard_map/reduce_scatter | solution.py:352
  889.7 598.5 %reduce-scatter.21.cloned.1.call-start = ((), (), s32[]{:S(2)}) async-start(), calls=%async_computation.21 | async-start | bytes 12976128 | tf_op jit(solution)/shard_map/reduce_scatter | solution.py:254
  896.5 753.1 %reduce-scatter.23.cloned.1.call-start = ((), (), s32[]{:S(2)}) async-start(), calls=%async_computation.22 | async-start | bytes 12976128 | tf_op jit(solution)/shard_map/reduce_scatter | solution.py:255
  903.9 931.4 %reduce-scatter.19.cloned.1.call-start = ((), (), s32[]{:S(2)}) async-start(), calls=%async_computation.20 | async-start | bytes 8650752 | tf_op jit(solution)/shard_map/reduce_scatter | solution.py:353
  909.7 1113.5 %reduce-scatter.13.cloned.1.call-start = ((), (), s32[]{:S(2)}) async-start(), calls=%async_computation.17 | async-start | bytes 8650752 | tf_op jit(solution)/shard_map/reduce_scatter | solution.py:350
  915.3 1270.4 %reduce-scatter.25.cloned.1.call-start = ((), (), s32[]{:S(2)}) async-start(), calls=%async_computation.23 | async-start | bytes 12976128
  (82 other events, 1627.8 us)
Sparse Core Ops, SparseCore 0:
  11.0 59.2 all-gather.10
  73.3 55.3 all-gather.16
  130.8 48.1 all-gather.12
  181.0 47.7 all-gather.18
  231.7 60.5 all-gather.14
  295.2 60.6 all-gather.20
  358.8 68.0 all-gather.22
  429.9 67.9 all-gather.24
  500.9 67.9 all-gather.26
  883.9 158.1 reduce-scatter.26
  1045.0 140.0 reduce-scatter.14
  1187.9 140.0 reduce-scatter.16
  1335.7 152.5 reduce-scatter.20
  1494.7 154.7 reduce-scatter.22
  1652.3 183.0 reduce-scatter.18
  1838.2 184.9 reduce-scatter.12
  2030.7 154.9 reduce-scatter.24
where the time goes:
time: 2200 us; the launch traced here: 2190 us
  waiting for transfers between devices  1750 us (80%)
  blocking collectives  132 us (6%)
  matrix products  113 us (5%)
  other arithmetic  72.5 us (3%)
  local copies, waits for them, and re-layouts  62.3 us (3%)
  starting transfers between devices  36.7 us (2%)
    unnamed x19, waiting for transfers between devices  203 us
    reduce_scatter x1, waiting for transfers between devices, shards(): lax.psum_scatter(grad_wq, ('dp', 'seq'), scatter_dimension=0, tiled=True)  188 us
    reduce_scatter x1, waiting for transfers between devices, shards(): lax.psum_scatter(grad_wo_turned, ('dp', 'seq'), scatter_dimension=0, tile...  186 us
    reduce_scatter x1, waiting for transfers between devices, shards(): lax.psum_scatter(grad_wu, ('dp', 'seq'), scatter_dimension=0, tiled=True)  161 us
    reduce_scatter x1, waiting for transfers between devices, shards(): lax.psum_scatter(grad_wg, ('dp', 'seq'), scatter_dimension=0, tiled=True)  160 us
    ppermute x24, waiting for transfers between devices, passed_along(): lax.ppermute(array, axis, [(i, (i + by) % length) for i in range(length)])  145 us
    reduce_scatter x1, waiting for transfers between devices, shards(): lax.psum_scatter(grad_wv, ('dp', 'seq'), scatter_dimension=0, tiled=True)  143 us
    reduce_scatter x1, waiting for transfers between devices, shards(): lax.psum_scatter(grad_wk, ('dp', 'seq'), scatter_dimension=0, tiled=True)  142 us
  transfers between devices with their start and end apart: 41, of which 40 were waited for; matrix products, arithmetic and copies ran while one was open for 6% of the time, Pallas kernels for 0%

commit v1 on v0

--- a/solution.py
+++ b/solution.py
@@ -3,6 +3,8 @@
 import jax
 import jax.numpy as jnp
 from jax import lax
+from jax.experimental import pallas as pl
+from jax.experimental.pallas import tpu as pltpu
 from jax.sharding import PartitionSpec as P
 
 eps_model = 1e-06
@@ -369,9 +371,409 @@
     )
 
 
+def dp_order():
+    order, bit = [0], lax.axis_size("dp") // 2
+    while bit:
+        order = order + [i ^ bit for i in order]
+        bit //= 2
+    return order
+
+
+def dp_swap(array, bit):
+    return lax.ppermute(array, "dp", [(i, i ^ bit) for i in range(lax.axis_size("dp"))])
+
+
+def dp_gather(array):
+    held, bit = array[None], lax.axis_size("dp") // 2
+    while bit:
+        held = jnp.concatenate([held, dp_swap(held, bit)], 0)
+        bit //= 2
+    return held
+
+
+def dp_scatter(partial):
+    bit = 1
+    while bit < lax.axis_size("dp"):
+        half = partial.shape[0] // 2
+        partial = partial[:half] + dp_swap(partial[half:].astype(jnp.bfloat16), bit).astype(
+            jnp.float32
+        )
+        bit *= 2
+    return partial[0]
+
+
+def to_seq(array):
+    return lax.all_to_all(array, "seq", 0, 0, tiled=True)
+
+
+def attend_kernel(query_ref, key_ref, value_ref, query_pos_ref, key_pos_ref, out_ref, low_ref, log_ref):
+    scale = query_ref.shape[-1] ** (-0.5)
+    scores = contract_cols(query_ref[...], key_ref[...]) * scale
+    allowed = key_pos_ref[...] <= query_pos_ref[...]
+    scores = jnp.where(allowed, scores, masked_value)
+    top = jnp.max(scores, axis=-1, keepdims=True)
+    weights = jnp.exp(scores - top)
+    total = jnp.sum(weights, axis=-1, keepdims=True)
+    probs = (weights * (1.0 / total)).astype(jnp.bfloat16)
+    attended = jnp.dot(probs, value_ref[...], preferred_element_type=jnp.float32)
+    out_ref[...] = attended
+    low_ref[...] = attended.astype(jnp.bfloat16)
+    log_ref[...] = top + jnp.log(total)
+
+
+def attend_back_kernel(
+    query_ref,
+    key_ref,
+    value_ref,
+    query_pos_ref,
+    key_pos_ref,
+    out_ref,
+    log_ref,
+    grad_ref,
+    grad_query_ref,
+    grad_key_ref,
+    grad_value_ref,
+):
+    @pl.when(pl.program_id(0) == 0)
+    def _():
+        grad_key_ref[...] = jnp.zeros_like(grad_key_ref)
+        grad_value_ref[...] = jnp.zeros_like(grad_value_ref)
+
+    scale = query_ref.shape[-1] ** (-0.5)
+    query, key, grad = query_ref[...], key_ref[...], grad_ref[...]
+    scores = contract_cols(query, key) * scale
+    allowed = key_pos_ref[...] <= query_pos_ref[...]
+    probs = jnp.where(allowed, jnp.exp(scores - log_ref[...]), 0.0)
+    delta = jnp.sum(grad.astype(jnp.float32) * out_ref[...], axis=-1, keepdims=True)
+    grad_probs = contract_cols(grad, value_ref[...])
+    grad_scores = (probs * (grad_probs - delta)).astype(jnp.bfloat16)
+    grad_value_ref[...] += contract_rows(probs.astype(jnp.bfloat16), grad)
+    grad_query_ref[...] = jnp.dot(grad_scores, key, preferred_element_type=jnp.float32) * scale
+    grad_key_ref[...] += contract_rows(grad_scores, query) * scale
+
+
+def attend_specs(rows, length, head_dim, block):
+    by_rows = pl.BlockSpec((block, head_dim), lambda i: (i, 0))
+    by_row = pl.BlockSpec((block, 1), lambda i: (i, 0))
+    whole = pl.BlockSpec((length, head_dim), lambda i: (0, 0))
+    key_pos = pl.BlockSpec((1, length), lambda i: (0, 0))
+    return (rows // block,), by_rows, by_row, whole, key_pos
+
+
+def attend(query, key, value, query_pos, key_pos):
+    rows, head_dim = query.shape
+    length = key.shape[0]
+    grid, by_rows, by_row, whole, keys = attend_specs(rows, length, head_dim, 512)
+    return pl.pallas_call(
+        attend_kernel,
+        grid=grid,
+        in_specs=[by_rows, whole, whole, by_row, keys],
+        out_specs=[by_rows, by_rows, by_row],
+        out_shape=[
+            jax.ShapeDtypeStruct((rows, head_dim), jnp.float32),
+            jax.ShapeDtypeStruct((rows, head_dim), jnp.bfloat16),
+            jax.ShapeDtypeStruct((rows, 1), jnp.float32),
+        ],
+        compiler_params=pltpu.CompilerParams(vmem_limit_bytes=40 * 1024 * 1024),
+    )(query, key, value, query_pos, key_pos)
+
+
+def attend_back(query, key, value, query_pos, key_pos, attended, log_total, grad):
+    rows, head_dim = query.shape
+    length = key.shape[0]
+    grid, by_rows, by_row, whole, keys = attend_specs(rows, length, head_dim, 512)
+    return pl.pallas_call(
+        attend_back_kernel,
+        grid=grid,
+        in_specs=[by_rows, whole, whole, by_row, keys, by_rows, by_row, by_rows],
+        out_specs=[by_rows, whole, whole],
+        out_shape=[
+            jax.ShapeDtypeStruct((rows, head_dim), jnp.float32),
+            jax.ShapeDtypeStruct((length, head_dim), jnp.float32),
+            jax.ShapeDtypeStruct((length, head_dim), jnp.float32),
+        ],
+        compiler_params=pltpu.CompilerParams(vmem_limit_bytes=48 * 1024 * 1024),
+    )(query, key, value, query_pos, key_pos, attended, log_total, grad)
+
+
+def rotate_rows(values, cosine, sine):
+    half_dim = values.shape[-1] // 2
+    turned = jnp.concatenate([-values[:, half_dim:], values[:, :half_dim]], -1)
+    return values * cosine + turned * sine
+
+
+def high_low(values):
+    high = values.astype(jnp.bfloat16)
+    return high, (values - high.astype(jnp.float32)).astype(jnp.bfloat16)
+
+
+def split_shards(
+    tokens,
+    span_order,
+    w_query,
+    key_matrix,
+    value_matrix,
+    w_output,
+    w_gate,
+    w_up,
+    w_down,
+    norm_gains,
+    head_gains,
+    cotangent,
+):
+    low, wide = jnp.bfloat16, jnp.float32
+    dp_size, seq_size = lax.axis_size("dp"), lax.axis_size("seq")
+    row_count, width = tokens.shape
+    head_dim = head_gains.shape[1]
+    kv_heads = key_matrix.shape[1] // head_dim
+    groups = w_query.shape[1] // key_matrix.shape[1]
+    own_heads = kv_heads // dp_size
+    pair_cols = groups * head_dim
+    query_cols, key_cols = own_heads * pair_cols, own_heads * head_dim
+    unit_cols = w_gate.shape[1] // dp_size
+    weight_rows = w_query.shape[0]
+    length = seq_size * row_count
+    all_rows = dp_size * row_count
+    span_len = row_count // 2
+    seq_index = lax.axis_index("seq")
+
+    def cut(weight):
+        return weight.reshape(weight_rows, dp_size, -1).transpose(1, 0, 2)
+
+    gain_cols = jnp.pad(norm_gains.T, ((0, 0), (0, 126)))
+    gain_cols = jnp.broadcast_to(gain_cols[None], (dp_size, weight_rows, 128))
+    first_part = jnp.concatenate(
+        [cut(w_query), cut(key_matrix), cut(value_matrix), cut(w_output.T), gain_cols], -1
+    )
+    second_part = jnp.concatenate([cut(w_gate), cut(w_up), cut(w_down.T)], -1)
+
+    def over_seq(part):
+        part = part.reshape(dp_size * weight_rows, -1)
+        return lax.all_gather(part, "seq", axis=0, tiled=True)
+
+    def by_width(gathered):
+        split = gathered.reshape(seq_size, dp_size, weight_rows, -1)
+        return split.transpose(1, 0, 2, 3).reshape(width, -1)
+
+    first_part = lax.all_to_all(first_part, "dp", 0, 0, tiled=True)
+    first_part = over_seq(first_part)
+    second_part = lax.all_to_all(second_part, "dp", 0, 0, tiled=True)
+    first_part, second_part = lax.optimization_barrier((first_part, second_part))
+    second_part = over_seq(second_part)
+    first_part = by_width(first_part)
+    qkv_cols = query_cols + 2 * key_cols
+    w_qkv = first_part[:, :qkv_cols]
+    wo_turned = first_part[:, qkv_cols : qkv_cols + query_cols]
+    gains = first_part[:, qkv_cols + query_cols :][:, :2].T.astype(wide)
+
+    all_tokens = dp_gather(tokens).reshape(all_rows, width)
+    orders = dp_gather(span_order[0])
+    own_slots = lax.dynamic_slice(orders, (0, 2 * seq_index), (dp_size, 2))
+    offsets = jnp.arange(span_len, dtype=jnp.int32)
+    row_pos = (own_slots[:, :, None] * span_len + offsets).reshape(all_rows)
+    cosine, sine = rope_tables(row_pos, head_dim)
+    gains_head = head_gains.astype(wide)
+    inputs = tokens.astype(wide)
+    all_inputs = all_tokens.astype(wide)
+    inverse = lax.rsqrt(jnp.mean(all_inputs * all_inputs, axis=-1, keepdims=True) + eps_model)
+    all_scaled = all_inputs * inverse
+    normed_low = (all_scaled * gains[0]).astype(low)
+    qkv_pre = jnp.dot(normed_low, w_qkv, preferred_element_type=wide)
+
+    def prepare(flat, gain):
+        return rotate_rows(rms_scale(flat, gain), cosine, sine)
+
+    def head_of(array, start, n):
+        return array[:, start + n * head_dim : start + (n + 1) * head_dim]
+
+    query_rot, query_back, key_rot, key_back = [], [], [], []
+    for n in range(own_heads * groups):
+        rotated, back = jax.vjp(prepare, head_of(qkv_pre, 0, n), gains_head[0])
+        query_rot.append(rotated.astype(low))
+        query_back.append(back)
+    for n in range(own_heads):
+        rotated, back = jax.vjp(prepare, head_of(qkv_pre, query_cols, n), gains_head[1])
+        key_rot.append(rotated.astype(low))
+        key_back.append(back)
+    value_low = qkv_pre[:, query_cols + key_cols :].astype(low)
+
+    def to_pairs(by_head):
+        stacked = jnp.stack([a.reshape(dp_size, row_count, -1) for a in by_head], 1)
+        return stacked.reshape(seq_size, row_count, -1)
+
+    def from_pairs(array):
+        split = array.reshape(dp_size, own_heads, row_count, -1)
+        return [split[:, n].reshape(all_rows, -1) for n in range(own_heads)]
+
+    pairs = to_seq(
+        to_pairs(
+            [
+                jnp.concatenate(
+                    query_rot[n * groups : (n + 1) * groups]
+                    + [key_rot[n], head_of(value_low, 0, n)],
+                    -1,
+                )
+                for n in range(own_heads)
+            ]
+        )
+    ).reshape(length, -1)
+
+    def heads_down(array):
+        return jnp.concatenate([head_of(array, 0, n) for n in range(groups)], 0)
+
+    def heads_across(array):
+        return jnp.concatenate([array[n * length : (n + 1) * length] for n in range(groups)], 1)
+
+    pair_query = heads_down(pairs[:, :pair_cols])
+    pair_key = pairs[:, pair_cols : pair_cols + head_dim]
+    pair_value = pairs[:, pair_cols + head_dim :]
+    pair_order = lax.dynamic_index_in_dim(orders, seq_index // own_heads, 0, keepdims=False)
+    pair_pos = (pair_order[:, None] * span_len + offsets).reshape(length)
+    query_pos = jnp.concatenate([pair_pos] * groups)[:, None]
+    key_pos = pair_pos[None, :]
+    attended, attended_low, log_total = attend(pair_query, pair_key, pair_value, query_pos, key_pos)
+    back_to_rows = to_seq(heads_across(attended_low).reshape(seq_size, row_count, pair_cols))
+    all_attended = jnp.concatenate(from_pairs(back_to_rows), -1)
+    partial = contract_cols(all_attended, wo_turned).reshape(dp_size, row_count, width)
+    middle = inputs + dp_scatter(partial)
+
+    second_part = by_width(second_part)
+    w_gate_up = second_part[:, : 2 * unit_cols]
+    wd_turned = second_part[:, 2 * unit_cols :]
+    normed_two, norm_two_back = jax.vjp(rms_scale, middle, gains[1])
+    normed_two_low = dp_gather(normed_two.astype(low)).reshape(all_rows, width)
+    all_cotangent = dp_gather(cotangent).reshape(all_rows, width)
+    gate_up = jnp.dot(normed_two_low, w_gate_up, preferred_element_type=wide)
+    hidden, swiglu_back = jax.vjp(swiglu, gate_up[:, :unit_cols], gate_up[:, unit_cols:])
+    hidden_low = hidden.astype(low)
+    grad_hidden = jnp.dot(all_cotangent, wd_turned, preferred_element_type=wide)
+    grad_gate, grad_up = swiglu_back(grad_hidden)
+    gate_up_low = jnp.concatenate([grad_gate.astype(low), grad_up.astype(low)], -1)
+    partial = contract_cols(gate_up_low, w_gate_up).reshape(dp_size, row_count, width)
+    grad_middle_norm, grad_gain_two = norm_two_back(dp_scatter(partial))
+    grad_middle = cotangent.astype(wide) + grad_middle_norm
+    middle_low = dp_gather(grad_middle.astype(low)).reshape(all_rows, width)
+    partial = contract_cols(hidden_low, wd_turned).reshape(dp_size, row_count, width)
+    output = middle + dp_scatter(partial)
+    grad_att = jnp.dot(middle_low, wo_turned, preferred_element_type=wide).astype(low)
+    pair_grad = to_seq(
+        to_pairs([grad_att[:, n * pair_cols : (n + 1) * pair_cols] for n in range(own_heads)])
+    ).reshape(length, pair_cols)
+
+    second_grads = jnp.concatenate(
+        [
+            contract_rows(normed_two_low, gate_up_low).astype(low),
+            contract_rows(all_cotangent, hidden_low).astype(low),
+            contract_rows(middle_low, all_attended).astype(low),
+        ],
+        -1,
+    )
+    second_grads = second_grads.reshape(dp_size, seq_size, weight_rows, -1).transpose(1, 0, 2, 3)
+    second_grads = second_grads.reshape(width, -1)
+    second_grads = lax.psum_scatter(second_grads, "seq", scatter_dimension=0, tiled=True)
+    second_grads = second_grads.reshape(dp_size, weight_rows, -1)
+    second_grads = lax.all_to_all(second_grads, "dp", 0, 0, tiled=True)
+
+    grad_query, grad_key, grad_value = attend_back(
+        pair_query,
+        pair_key,
+        pair_value,
+        query_pos,
+        key_pos,
+        attended,
+        log_total,
+        heads_down(pair_grad),
+    )
+    grad_pairs = jnp.concatenate(
+        [heads_across(grad_query.astype(low)), grad_key.astype(low), grad_value.astype(low)], -1
+    )
+    grad_pairs = from_pairs(to_seq(grad_pairs.reshape(seq_size, row_count, -1)))
+    grad_query_pre, grad_key_pre, grad_value_low = [], [], []
+    gain_query, gain_key = 0.0, 0.0
+    for n in range(own_heads):
+        for g in range(groups):
+            turned = head_of(grad_pairs[n], 0, g).astype(wide)
+            before, gain = query_back[n * groups + g](turned)
+            grad_query_pre.append(before.astype(low))
+            gain_query = gain_query + gain
+        before, gain = key_back[n](head_of(grad_pairs[n], pair_cols, 0).astype(wide))
+        grad_key_pre.append(before.astype(low))
+        gain_key = gain_key + gain
+        grad_value_low.append(grad_pairs[n][:, pair_cols + head_dim :])
+    grad_qkv = jnp.concatenate(grad_query_pre + grad_key_pre + grad_value_low, -1)
+    first_grads = contract_rows(normed_low, grad_qkv).astype(low)
+    partial = contract_cols(grad_qkv, w_qkv)
+    grad_gain_one = jnp.sum(partial * all_scaled, axis=0)
+    grad_normed = dp_scatter(partial.reshape(dp_size, row_count, width))
+    _, norm_back = jax.vjp(lambda values: rms_scale(values, gains[0]), inputs)
+    grad_input = grad_middle + norm_back(grad_normed)[0]
+
+    devices = dp_size * seq_size
+    blocks = qkv_cols // 128
+    first_grads = first_grads.reshape(devices, weight_rows, blocks, 128).transpose(0, 2, 1, 3)
+    norm_parts = jnp.stack(
+        [
+            part.reshape(devices, weight_rows)
+            for gain in (grad_gain_one, grad_gain_two)
+            for part in high_low(gain)
+        ],
+        1,
+    ).reshape(devices, -1, 128)
+    head_parts = jnp.stack([part for gain in (gain_query, gain_key) for part in high_low(gain)])
+    head_parts = jnp.broadcast_to(head_parts[None], (devices,) + head_parts.shape)
+    gain_parts = jnp.concatenate([norm_parts, head_parts], 1)
+    gain_rows = gain_parts.shape[1]
+    gain_parts = jnp.pad(gain_parts, ((0, 0), (0, -gain_rows % 16), (0, 0)))
+    sent = jnp.concatenate([first_grads.reshape(devices, -1, 128), gain_parts], 1)
+    taken = lax.all_to_all(sent, ("dp", "seq"), 0, 0, tiled=True)
+    split_at = blocks * weight_rows
+    gain_parts = jnp.sum(taken[:, split_at : split_at + gain_rows].astype(wide), 0)
+    norm_rows = gain_rows - 4
+    grad_norm = gain_parts[:norm_rows].reshape(2, 2, weight_rows).sum(1)
+    grad_head = gain_parts[norm_rows:].reshape(2, 2, head_dim).sum(1)
+    first_grads = taken[:, :split_at].reshape(dp_size, seq_size, blocks, weight_rows, 128)
+    first_grads = jnp.sum(first_grads.astype(wide), 1)
+
+    def joined(start, cols):
+        part = first_grads[:, start // 128 : (start + cols) // 128]
+        return part.transpose(2, 0, 1, 3).reshape(weight_rows, -1)
+
+    def joined_second(start, cols):
+        part = second_grads[:, :, start : start + cols].astype(wide)
+        return part.transpose(1, 0, 2).reshape(weight_rows, -1)
+
+    return (
+        output.astype(low),
+        grad_input.astype(low),
+        joined(0, query_cols),
+        joined(query_cols, key_cols),
+        joined(query_cols + key_cols, key_cols),
+        joined_second(3 * unit_cols, query_cols).T,
+        joined_second(0, unit_cols),
+        joined_second(unit_cols, unit_cols),
+        joined_second(2 * unit_cols, unit_cols).T,
+        grad_norm,
+        grad_head,
+    )
+
+
 def solution(mesh):
+    sizes = dict(mesh.shape)
+
+    def layer(*arrays):
+        query_cols, key_cols = arrays[2].shape[1], arrays[3].shape[1]
+        kv_heads = key_cols // arrays[10].shape[1]
+        dp, seq = sizes["dp"], sizes["seq"]
+        fits = dp & (dp - 1) == 0 and kv_heads % dp == 0 and kv_heads == seq
+        fits = fits and arrays[6].shape[1] % (128 * dp) == 0
+        return mapped(split_shards if fits else shards, mesh)(*arrays)
+
+    return layer
+
+
+def mapped(function, mesh):
     return jax.shard_map(
-        shards,
+        function,
         mesh=mesh,
         in_specs=(
             P(("dp", "seq"), None),

time: 2200 us -> 473 us (0.21)
  waiting for transfers between devices: 1750 us -> 263 us
  matrix products: 113 us -> 26.3 us
  blocking collectives: 132 us -> 62.1 us
  other arithmetic: 72.5 us -> 25.7 us
  local copies, waits for them, and re-layouts: 62.3 us -> 34.8 us
    reduce_scatter x6 -> x1, waiting for transfers between devices: 980 us -> 36.6 us  [split_shards(): lax.psum_scatter(second_grads, 'seq', scatter_dimension=0, tiled=True)]
    all_gather x9 -> x2, waiting for transfers between devices: 417 us -> 40.5 us  [over_seq(): return lax.all_gather(part, 'seq', axis=0, tiled=True)]
    unnamed x19 -> x3, waiting for transfers between devices: 203 us -> 0.05 us
    all_to_all x0 -> x5, waiting for transfers between devices: none -> 120 us  [the longest x2 64.8 us: to_seq(): return lax.all_to_all(array, 'seq', 0, 0, tiled=True)]
    ppermute x24 -> x18, waiting for transfers between devices: 145 us -> 66.1 us  [dp_swap(): lax.ppermute(array, 'dp', [(i, i ^ bit) for i in range(lax.axis_size('dp'...]
    all_gather x1 -> x0, blocking collectives: 69.5 us -> none  [shards(): lax.all_gather(norm_gains, ('dp', 'seq'), axis=1, tiled=True)]
    psum x1 -> x0, blocking collectives: 63 us -> none  [shards(): lax.psum(jnp.stack([grad_gain_query, grad_gain_key]), ('dp', 'seq'))]
    all_to_all x0 -> x3, blocking collectives: none -> 62.1 us  [the longest x2 50.2 us: to_seq(): return lax.all_to_all(array, 'seq', 0, 0, tiled=True)]
  transfers between devices with their start and end apart: 41 -> 26, of which waited for: 40 -> 20; matrix products, arithmetic and copies ran while one was open for 6% -> 11% of each run, Pallas kernels for 0% -> 1%
where the time goes in v1:
time: 473 us; the launch traced here: 472 us
  waiting for transfers between devices  263 us (56%)
  blocking collectives  62.1 us (13%)
  local copies, waits for them, and re-layouts  34.8 us (7%)
  starting transfers between devices  29.7 us (6%)
  matrix products  26.3 us (6%)
  other arithmetic  25.7 us (5%)
  Pallas kernels  15.4 us (3%)
  between operations  15.2 us (3%)
    ppermute x18, waiting for transfers between devices, dp_swap(): lax.ppermute(array, 'dp', [(i, i ^ bit) for i in range(lax.axis_size('dp'...  66.1 us
    all_to_all x2, waiting for transfers between devices, to_seq(): return lax.all_to_all(array, 'seq', 0, 0, tiled=True)  64.8 us
    all_to_all x2, blocking collectives, to_seq(): return lax.all_to_all(array, 'seq', 0, 0, tiled=True)  50.2 us
    all_to_all x1, waiting for transfers between devices, split_shards(): taken = lax.all_to_all(sent, ('dp', 'seq'), 0, 0, tiled=True)  50 us
    all_gather x2, waiting for transfers between devices, over_seq(): return lax.all_gather(part, 'seq', axis=0, tiled=True)  40.5 us
    reduce_scatter x1, waiting for transfers between devices, split_shards(): lax.psum_scatter(second_grads, 'seq', scatter_dimension=0, tiled=True)  36.6 us
    ppermute x18, starting transfers between devices, dp_swap(): lax.ppermute(array, 'dp', [(i, i ^ bit) for i in range(lax.axis_size('dp'...  12.2 us
    all_to_all x1, blocking collectives, split_shards(): first_part = lax.all_to_all(first_part, 'dp', 0, 0, tiled=True)  11.9 us
  transfers between devices with their start and end apart: 26, of which 20 were waited for; matrix products, arithmetic and copies ran while one was open for 11% of the time, Pallas kernels for 1%

profile of v1, /device:TPU:0, one launch (start us, length us, event | category | flops | bytes accessed | tf_op | source)
XLA Modules:
  0.0 472.3 jit_solution(17544915251576892011)
XLA Ops:
  12.2 11.9 %all_to_all.40 = bf16[4,32,1664]{2,1,0:T(8,128)(2,1)} all-to-all(bf16[4,32,1664]{2,1,0:T(8,128)(2,1)S(1)} %copy.85), channel_id=1, replica_groups=mesh['dp'=4,'seq'=8] {'dp'}, dimensions={0} | all-to-all | bytes 851968 | tf_op jit(solution)/shard_map/all_to_all | solution.py:558
  25.7 3.5 all-to-all-start.1
  31.4 13.0 %collective-permute-done.2 = s32[1,16]{1,0:T(1,128)S(1)} collective-permute-done((s32[1,16]{1,0:T(1,128)S(1)}, s32[1,16]{1,0:T(1,128)S(1)}, u32[]{:S(2)}, u32[]{:S(2)}) %collective-permute-start.2) | collective-permute-done | bytes 96 | tf_op jit(solution)/shard_map/ppermute | solution.py:383
  48.0 40.5 %all-gather.3.cloned.1.call-done = bf16[1024,1664]{1,0:T(8,128)(2,1)} async-done(((bf16[128,1664]{1,0:T(8,128)(2,1)}), bf16[1024,1664]{1,0:T(8,128)(2,1)}) %all-gather.3.cloned.1.call-update) | async-done | bytes 3407888 | tf_op jit(solution)/shard_map/all_gather | solution.py:552
  103.7 3.6 all-to-all-start.2
  107.9 43.4 %all-to-all-done.2 = bf16[8,128,512]{2,1,0:T(8,128)(2,1)S(1)} async-done(((bf16[8,128,512]{2,1,0:T(8,128)(2,1)}), bf16[8,128,512]{2,1,0:T(8,128)(2,1)S(1)}, u32[]{:S(2)}, u32[]{:S(2)}) %all-to-all-start.2) | async-done | bytes 1048608 | tf_op jit(solution)/shard_map/all_to_all | solution.py:406
  151.5 6.8 %shard_map.203 = (f32[2048,128]{1,0:T(8,128)S(1)}, bf16[2048,128]{1,0:T(8,128)(2,1)S(1)}, f32[2048,1]{1,0:T(8,128)S(1)}) custom-call(bf16[2048,128]{1,0:T(8,128)(2,1)S(1)} %pad_maximum_fusion.15.query_ref, bf16[1024,128]{1,0:T(8,128)(2,1)S(1)} %get-tuple-element.85.key_ref, bf16[1024,128]{1,0:T(8,128)(2,1)S(1)} %get-tuple-element.84.value_ref, ...), custom_call_target="tpu_custom_call" | custom-call | tf_op jit(solution)/shard_map/pallas_call | solution.py:467
  158.5 32.6 %all_to_all.41 = bf16[8,128,256]{2,1,0:T(8,128)(2,1)S(1)} all-to-all(bf16[8,128,256]{2,1,0:T(8,128)(2,1)S(1)} %bitcast.214), channel_id=1, replica_groups=mesh['dp'=4,'seq'=8] {'seq'}, dimensions={0} | all-to-all | bytes 1048576 | tf_op jit(solution)/shard_map/all_to_all | solution.py:406
  197.7 7.1 %collective-permute-done.5 = bf16[1,128,1024]{2,1,0:T(8,128)(2,1)S(1)} collective-permute-done((bf16[1,128,1024]{2,1,0:T(8,128)(2,1)S(1)}, bf16[1,128,1024]{2,1,0:T(8,128)(2,1)S(1)}, u32[]{:S(2)}, u32[]{:S(2)}) %collective-permute-start.5) | collective-permute-done | bytes 262176 | tf_op jit(solution)/shard_map/ppermute | solution.py:383
  210.6 4.7 collective-permute-done.6
  232.3 6.8 %collective-permute-done.13 = bf16[1,128,1024]{2,1,0:T(8,128)(2,1)S(1)} collective-permute-done((bf16[1,128,1024]{2,1,0:T(8,128)(2,1)S(1)}, bf16[1,128,1024]{2,1,0:T(8,128)(2,1)S(1)}, u32[]{:S(2)}, u32[]{:S(2)}) %collective-permute-start.13) | collective-permute-done | bytes 262176 | tf_op jit(solution)/shard_map/ppermute | solution.py:383
  239.4 4.9 %collective-permute-done.9 = bf16[1,128,1024]{2,1,0:T(8,128)(2,1)S(1)} collective-permute-done((bf16[1,128,1024]{2,1,0:T(8,128)(2,1)S(1)}, bf16[1,128,1024]{2,1,0:T(8,128)(2,1)S(1)}, u32[]{:S(2)}, u32[]{:S(2)}) %collective-permute-start.9) | collective-permute-done | bytes 262176 | tf_op jit(solution)/shard_map/ppermute | solution.py:383
  246.9 6.3 %collective-permute-done.14 = bf16[1,128,1024]{2,1,0:T(8,128)(2,1)S(1)} collective-permute-done((bf16[1,128,1024]{2,1,0:T(8,128)(2,1)S(1)}, bf16[1,128,1024]{2,1,0:T(8,128)(2,1)S(1)}, u32[]{:S(2)}, u32[]{:S(2)}) %collective-permute-start.14) | collective-permute-done | bytes 262176 | tf_op jit(solution)/shard_map/ppermute | solution.py:383
  257.8 17.6 %all_to_all.42 = bf16[8,128,256]{2,1,0:T(8,128)(2,1)S(1)} all-to-all(bf16[8,128,256]{2,1,0:T(8,128)(2,1)S(1)} %bitcast.215), channel_id=1, replica_groups=mesh['dp'=4,'seq'=8] {'seq'}, dimensions={0} | all-to-all | bytes 1048576 | tf_op jit(solution)/shard_map/all_to_all | solution.py:406
  275.5 8.5 %shard_map.204 = (f32[2048,128]{1,0:T(8,128)S(1)}, f32[1024,128]{1,0:T(8,128)S(1)}, f32[1024,128]{1,0:T(8,128)S(1)}) custom-call(bf16[2048,128]{1,0:T(8,128)(2,1)S(1)} %pad_maximum_fusion.15.query_ref, bf16[1024,128]{1,0:T(8,128)(2,1)S(1)} %get-tuple-element.85.key_ref, bf16[1024,128]{1,0:T(8,128)(2,1)S(1)} %get-tuple-element.84.value_ref, ...), custom_call_target="tpu_custom_call" | custom-call | tf_op jit(solution)/shard_map/pallas_call | solution.py:485
  285.3 3.6 all-to-all-start.5
  291.9 3.6 convolution_convert_fusion
  301.4 21.5 %all-to-all-done.5 = bf16[8,128,512]{2,1,0:T(8,128)(2,1)S(1)} async-done(((bf16[8,128,512]{2,1,0:T(8,128)(2,1)}), bf16[8,128,512]{2,1,0:T(8,128)(2,1)S(1)}, u32[]{:S(2)}, u32[]{:S(2)}) %all-to-all-start.5) | async-done | bytes 1048608 | tf_op jit(solution)/shard_map/all_to_all | solution.py:406
  337.3 3.0 all-to-all-start.6
  345.4 13.7 %collective-permute-done.17 = bf16[1,128,1024]{2,1,0:T(8,128)(2,1)S(1)} collective-permute-done((bf16[1,128,1024]{2,1,0:T(8,128)(2,1)S(1)}, bf16[1,128,1024]{2,1,0:T(8,128)(2,1)S(1)}, u32[]{:S(2)}, u32[]{:S(2)}) %collective-permute-start.17) | collective-permute-done | bytes 262176 | tf_op jit(solution)/shard_map/ppermute | solution.py:383
  360.3 50.0 %all-to-all-done.6 = bf16[32,272,128]{2,1,0:T(8,128)(2,1)S(1)} async-done(((bf16[32,272,128]{2,1,0:T(8,128)(2,1)}), bf16[32,272,128]{2,1,0:T(8,128)(2,1)S(1)}, u32[]{:S(2)}, u32[]{:S(2)}) %all-to-all-start.6) | async-done | bytes 2228256 | tf_op jit(solution)/shard_map/all_to_all | solution.py:728
  411.6 36.6 %reduce-scatter.2.cloned.1.call-done = bf16[128,2816]{1,0:T(8,128)(2,1)} async-done(((bf16[1024,2816]{1,0:T(8,128)(2,1)}), bf16[128,2816]{1,0:T(8,128)(2,1)}) %reduce-scatter.2.cloned.1.call-update) | async-done | bytes 720912 | tf_op jit(solution)/shard_map/reduce_scatter | solution.py:673
  448.2 3.5 all-to-all-start.7
  457.7 4.9 %all-to-all-done.7 = bf16[4,32,2816]{2,1,0:T(8,128)(2,1)S(1)} async-done(((bf16[4,32,2816]{2,1,0:T(8,128)(2,1)}), bf16[4,32,2816]{2,1,0:T(8,128)(2,1)S(1)}, u32[]{:S(2)}, u32[]{:S(2)}) %all-to-all-start.7) | async-done | bytes 720928 | tf_op jit(solution)/shard_map/all_to_all | solution.py:675
  (315 shorter events, 105.5 us)
Async XLA Ops:
  7.2 81.3 %all-gather.3.cloned.1.call-start = ((), (), s32[]{:S(2)}) async-start(), calls=%async_computation.9 | async-start | bytes 3833856 | tf_op jit(solution)/shard_map/all_gather | solution.py:552
  25.7 22.2 %all-to-all-start.1 = ((bf16[4,32,2304]{2,1,0:T(8,128)(2,1)}), bf16[4,32,2304]{2,1,0:T(8,128)(2,1)S(1)}, u32[]{:S(2)}, u32[]{:S(2)}) async-start(bf16[4,32,2304]{2,1,0:T(8,128)(2,1)} %copy.86), calls=%async_computation.1 | async-start | bytes 1179648 | tf_op jit(solution)/shard_map/all_to_all | solution.py:560
  29.2 189.2 %all-gather.5.cloned.1.call-start = ((), (), s32[]{:S(2)}) async-start(), calls=%async_computation.10 | async-start | bytes 5308416 | tf_op jit(solution)/shard_map/all_gather | solution.py:552
  29.3 16.4 %collective-permute-start = (bf16[1,128,1024]{2,1,0:T(8,128)(2,1)S(1)}, bf16[1,128,1024]{2,1,0:T(8,128)(2,1)S(1)}, u32[]{:S(2)}, u32[]{:S(2)}) collective-permute-start(bf16[1,128,1024]{2,1,0:T(8,128)(2,1)S(1)} %bitcast.175), channel_id=1, source_target_pairs={{0,16},{8,24},{16,0},{24,8},{1,17},{9,25},{17,1},{25,9},{2,18},{10... | collective-permute-start | bytes 786440 | tf_op jit(solution)/shard_map/ppermute | solution.py:383
  31.2 13.2 %collective-permute-start.2 = (s32[1,16]{1,0:T(1,128)S(1)}, s32[1,16]{1,0:T(1,128)S(1)}, u32[]{:S(2)}, u32[]{:S(2)}) collective-permute-start(s32[1,16]{1,0:T(1,128)S(1)} %copy-done.40), channel_id=1, source_target_pairs={{0,16},{8,24},{16,0},{24,8},{1,17},{9,25},{17,1},{25,9},{2,18},{10... | collective-permute-start | bytes 200 | tf_op jit(solution)/shard_map/ppermute | solution.py:383
  45.7 2.0 collective-permute-start.1
  103.7 47.6 %all-to-all-start.2 = ((bf16[8,128,512]{2,1,0:T(8,128)(2,1)}), bf16[8,128,512]{2,1,0:T(8,128)(2,1)S(1)}, u32[]{:S(2)}, u32[]{:S(2)}) async-start(bf16[8,128,512]{2,1,0:T(8,128)(2,1)} %bitcast.23), calls=%async_computation.2 | async-start | bytes 2097152 | tf_op jit(solution)/shard_map/all_to_all | solution.py:406
  193.4 2.0 collective-permute-start.4
  195.6 9.2 %collective-permute-start.5 = (bf16[1,128,1024]{2,1,0:T(8,128)(2,1)S(1)}, bf16[1,128,1024]{2,1,0:T(8,128)(2,1)S(1)}, u32[]{:S(2)}, u32[]{:S(2)}) collective-permute-start(bf16[1,128,1024]{2,1,0:T(8,128)(2,1)S(1)} %slice.591), channel_id=1, source_target_pairs={{0,16},{8,24},{16,0},{24,8},{1,17},{9,25},{17,1},{25,9},{2,18},{10... | collective-permute-start | bytes 786440 | tf_op jit(solution)/shard_map/ppermute | solution.py:383
  197.1 13.3 %collective-permute-start.10 = (bf16[1,128,1024]{2,1,0:T(8,128)(2,1)S(1)}, bf16[1,128,1024]{2,1,0:T(8,128)(2,1)S(1)}, u32[]{:S(2)}, u32[]{:S(2)}) collective-permute-start(bf16[1,128,1024]{2,1,0:T(8,128)(2,1)S(1)} %bitcast.209), channel_id=1, source_target_pairs={{0,16},{8,24},{16,0},{24,8},{1,17},{9,25},{17,1},{25,9},{2,18},{10... | collective-permute-start | bytes 786440 | tf_op jit(solution)/shard_map/ppermute | solution.py:383
  205.9 9.3 %collective-permute-start.6 = (bf16[1,128,1024]{2,1,0:T(8,128)(2,1)S(1)}, bf16[1,128,1024]{2,1,0:T(8,128)(2,1)S(1)}, u32[]{:S(2)}, u32[]{:S(2)}) collective-permute-start(bf16[1,128,1024]{2,1,0:T(8,128)(2,1)S(1)} %fusion.49), channel_id=1, source_target_pairs={{0,16},{8,24},{16,0},{24,8},{1,17},{9,25},{17,1},{25,9},{2,18},{10... | collective-permute-start | bytes 786440 | tf_op jit(solution)/shard_map/ppermute | solution.py:383
  210.5 4.9 %collective-permute-start.11 = (bf16[2,128,1024]{2,1,0:T(8,128)(2,1)S(1)}, bf16[2,128,1024]{2,1,0:T(8,128)(2,1)S(1)}, u32[]{:S(2)}, u32[]{:S(2)}) collective-permute-start(bf16[2,128,1024]{2,1,0:T(8,128)(2,1)S(1)} %pad_maximum_fusion.19), channel_id=1, source_target_pairs={{0,8},{8,0},{16,24},{24,16},{1,9},{9,1},{17,25},{25,17},{2,10},{10... | collective-permute-start | bytes 1572872 | tf_op jit(solution)/shard_map/ppermute | solution.py:383
  215.3 2.0 collective-permute-start.7
  226.6 2.6 collective-permute-start.12
  227.9 3.6 collective-permute-start.8
  229.9 9.2 %collective-permute-start.13 = (bf16[1,128,1024]{2,1,0:T(8,128)(2,1)S(1)}, bf16[1,128,1024]{2,1,0:T(8,128)(2,1)S(1)}, u32[]{:S(2)}, u32[]{:S(2)}) collective-permute-start(bf16[1,128,1024]{2,1,0:T(8,128)(2,1)S(1)} %slice.589), channel_id=1, source_target_pairs={{0,16},{8,24},{16,0},{24,8},{1,17},{9,25},{17,1},{25,9},{2,18},{10... | collective-permute-start | bytes 786440 | tf_op jit(solution)/shard_map/ppermute | solution.py:383
  231.7 12.6 %collective-permute-start.9 = (bf16[1,128,1024]{2,1,0:T(8,128)(2,1)S(1)}, bf16[1,128,1024]{2,1,0:T(8,128)(2,1)S(1)}, u32[]{:S(2)}, u32[]{:S(2)}) collective-permute-start(bf16[1,128,1024]{2,1,0:T(8,128)(2,1)S(1)} %slice.590), channel_id=1, source_target_pairs={{0,16},{8,24},{16,0},{24,8},{1,17},{9,25},{17,1},{25,9},{2,18},{10... | collective-permute-start | bytes 786440 | tf_op jit(solution)/shard_map/ppermute | solution.py:383
  245.4 7.8 %collective-permute-start.14 = (bf16[1,128,1024]{2,1,0:T(8,128)(2,1)S(1)}, bf16[1,128,1024]{2,1,0:T(8,128)(2,1)S(1)}, u32[]{:S(2)}, u32[]{:S(2)}) collective-permute-start(bf16[1,128,1024]{2,1,0:T(8,128)(2,1)S(1)} %get-tuple-element.67), channel_id=1, source_target_pairs={{0,16},{8,24},{16,0},{24,8},{1,17},{9,25},{17,1},{25,9},{2,18},{10... | collective-permute-start | bytes 786440 | tf_op jit(solution)/shard_map/ppermute | solution.py:383
  253.2 2.0 collective-permute-start.15
  285.3 37.5 %all-to-all-start.5 = ((bf16[8,128,512]{2,1,0:T(8,128)(2,1)}), bf16[8,128,512]{2,1,0:T(8,128)(2,1)S(1)}, u32[]{:S(2)}, u32[]{:S(2)}) async-start(bf16[8,128,512]{2,1,0:T(8,128)(2,1)} %bitcast.55), calls=%async_computation.5 | async-start | bytes 2097152 | tf_op jit(solution)/shard_map/all_to_all | solution.py:406
  289.0 159.2 %reduce-scatter.2.cloned.1.call-start = ((), (), s32[]{:S(2)}) async-start(), calls=%async_computation.11 | async-start | bytes 6488064 | tf_op jit(solution)/shard_map/reduce_scatter | solution.py:673
  337.3 72.9 %all-to-all-start.6 = ((bf16[32,272,128]{2,1,0:T(8,128)(2,1)}), bf16[32,272,128]{2,1,0:T(8,128)(2,1)S(1)}, u32[]{:S(2)}, u32[]{:S(2)}) async-start(bf16[32,272,128]{2,1,0:T(8,128)(2,1)} %pad_maximum_fusion.1), calls=%async_computation.6 | async-start | bytes 4456448 | tf_op jit(solution)/shard_map/all_to_all | solution.py:728
  343.9 15.2 %collective-permute-start.17 = (bf16[1,128,1024]{2,1,0:T(8,128)(2,1)S(1)}, bf16[1,128,1024]{2,1,0:T(8,128)(2,1)S(1)}, u32[]{:S(2)}, u32[]{:S(2)}) collective-permute-start(bf16[1,128,1024]{2,1,0:T(8,128)(2,1)S(1)} %slice.588), channel_id=1, source_target_pairs={{0,16},{8,24},{16,0},{24,8},{1,17},{9,25},{17,1},{25,9},{2,18},{10... | collective-permute-start | bytes 786440 | tf_op jit(solution)/shard_map/ppermute | solution.py:383
  448.2 14.4 %all-to-all-start.7 = ((bf16[4,32,2816]{2,1,0:T(8,128)(2,1)}), bf16[4,32,2816]{2,1,0:T(8,128)(2,1)S(1)}, u32[]{:S(2)}, u32[]{:S(2)}) async-start(bf16[4,32,2816]{2,1,0:T(8,128)(2,1)} %bitcast.234), calls=%async_computation.8 | async-start | bytes 1441792 | tf_op jit(solution)/shard_map/all_to_all | solution.py:675
  (51 other events, 438.8 us)
Sparse Core Ops, SparseCore 0:
  24.2 64.2 all-gather.2
  99.1 107.5 all-gather.4
  301.5 146.6 reduce-scatter.1

commit v2 on v0

--- a/solution.py
+++ b/solution.py
@@ -3,6 +3,8 @@
 import jax
 import jax.numpy as jnp
 from jax import lax
+from jax.experimental import pallas as pl
+from jax.experimental.pallas import tpu as pltpu
 from jax.sharding import PartitionSpec as P
 
 eps_model = 1e-06
@@ -369,9 +371,436 @@
     )
 
 
+def swapped(array, axis, by):
+    return lax.ppermute(array, axis, [(i, i ^ by) for i in range(lax.axis_size(axis))])
+
+
+def over_dp(array):
+    return lax.all_to_all(array, "dp", 0, 0, tiled=True)
+
+
+def gathered(array, axis):
+    return lax.all_gather(array, axis, axis=0, tiled=True)
+
+
+def summed(array, axis):
+    return lax.psum_scatter(array, axis, scatter_dimension=0, tiled=True)
+
+
+def gather_seq(rows):
+    count, place = lax.axis_size("seq"), lax.axis_index("seq")
+    row_count = rows.shape[0]
+    blocks = [rows, None]
+    for n in range(2, count, 2):
+        blocks += [swapped(rows, "seq", n), None]
+    for n in range(0, count, 2):
+        blocks[n + 1] = swapped(blocks[n], "seq", 1)
+    held = jnp.zeros((count * row_count,) + rows.shape[1:], rows.dtype)
+    for n, block in enumerate(blocks):
+        held = lax.dynamic_update_slice_in_dim(held, block, (place ^ n) * row_count, 0)
+    return held
+
+
+def scatter_seq(partial):
+    low, wide = jnp.bfloat16, jnp.float32
+    count, place = lax.axis_size("seq"), lax.axis_index("seq")
+    row_count = partial.shape[0] // count
+
+    def block(n):
+        return lax.dynamic_slice_in_dim(partial, (place ^ n) * row_count, row_count)
+
+    order = list(reversed(range(0, count, 2)))
+    arrived = [swapped(block(n + 1).astype(low), "seq", 1) for n in order]
+    sums = []
+    for k, n in enumerate(order):
+        if k:
+            held = lax.optimization_barrier((arrived[k], *sums[-2:]))
+            arrived[k], sums[-2:] = held[0], held[1:]
+        pair = block(n) + arrived[k].astype(wide)
+        if k:
+            sums[-1] = swapped(sums[-1], "seq", order[k - 1])
+        sums.append(pair.astype(low) if n else pair)
+    total = sums[-1]
+    for other in sums[:-1]:
+        total = total + other.astype(wide)
+    return total
+
+
+def gather_dp(array):
+    size, place = lax.axis_size("dp"), lax.axis_index("dp")
+    rows, bit = array.shape[0], size // 2
+    held = jnp.zeros((size * rows,) + array.shape[1:], array.dtype)
+    blocks, order = array, [0]
+    while bit:
+        blocks = jnp.concatenate([blocks, swapped(blocks, "dp", bit)], 0)
+        order = order + [n ^ bit for n in order]
+        bit //= 2
+    for k, n in enumerate(order):
+        block = blocks[k * rows : (k + 1) * rows]
+        held = lax.dynamic_update_slice_in_dim(held, block, (place ^ n) * rows, 0)
+    return held
+
+
+def gather_team(rows):
+    bit = lax.axis_size("dp") // 2
+    while bit:
+        rows = jnp.concatenate([rows, swapped(rows, "dp", bit)], 0)
+        bit //= 2
+    return rows
+
+
+def scatter_step(partial, bit):
+    half = partial.shape[0] // 2
+    other = swapped(partial[half:].astype(jnp.bfloat16), "dp", bit)
+    return partial[:half] + other.astype(jnp.float32)
+
+
+def scatter_rest(partial):
+    bit = 2
+    while bit < lax.axis_size("dp"):
+        partial = scatter_step(partial, bit)
+        bit *= 2
+    return partial
+
+
+def sum_row_halves(array, axis, bit):
+    mine = ((lax.axis_index(axis) & bit) != 0).astype(jnp.int32)
+    half = array.shape[0] // 2
+    other = lax.dynamic_slice_in_dim(array, (1 - mine) * half, half).astype(jnp.bfloat16)
+    kept = lax.dynamic_slice_in_dim(array, mine * half, half)
+    return kept.astype(jnp.float32) + swapped(other, axis, bit).astype(jnp.float32)
+
+
+def to_seq(array):
+    return lax.all_to_all(array, "seq", 0, 0, tiled=True)
+
+
+def attend_kernel(query_ref, key_ref, value_ref, query_pos_ref, key_pos_ref, out_ref, low_ref, log_ref):
+    scale = query_ref.shape[-1] ** (-0.5)
+    scores = contract_cols(query_ref[...], key_ref[...]) * scale
+    allowed = key_pos_ref[...] <= query_pos_ref[...]
+    scores = jnp.where(allowed, scores, masked_value)
+    top = jnp.max(scores, axis=-1, keepdims=True)
+    weights = jnp.exp(scores - top)
+    total = jnp.sum(weights, axis=-1, keepdims=True)
+    probs = (weights * (1.0 / total)).astype(jnp.bfloat16)
+    attended = jnp.dot(probs, value_ref[...], preferred_element_type=jnp.float32)
+    out_ref[...] = attended
+    low_ref[...] = attended.astype(jnp.bfloat16)
+    log_ref[...] = top + jnp.log(total)
+
+
+def attend_back_kernel(
+    query_ref,
+    key_ref,
+    value_ref,
+    query_pos_ref,
+    key_pos_ref,
+    out_ref,
+    log_ref,
+    grad_ref,
+    grad_query_ref,
+    grad_key_ref,
+    grad_value_ref,
+):
+    @pl.when(pl.program_id(0) == 0)
+    def _():
+        grad_key_ref[...] = jnp.zeros_like(grad_key_ref)
+        grad_value_ref[...] = jnp.zeros_like(grad_value_ref)
+
+    scale = query_ref.shape[-1] ** (-0.5)
+    query, key, grad = query_ref[...], key_ref[...], grad_ref[...]
+    scores = contract_cols(query, key) * scale
+    allowed = key_pos_ref[...] <= query_pos_ref[...]
+    probs = jnp.where(allowed, jnp.exp(scores - log_ref[...]), 0.0)
+    delta = jnp.sum(grad.astype(jnp.float32) * out_ref[...], axis=-1, keepdims=True)
+    grad_probs = contract_cols(grad, value_ref[...])
+    grad_scores = (probs * (grad_probs - delta)).astype(jnp.bfloat16)
+    grad_value_ref[...] += contract_rows(probs.astype(jnp.bfloat16), grad)
+    grad_query_ref[...] = jnp.dot(grad_scores, key, preferred_element_type=jnp.float32) * scale
+    grad_key_ref[...] += contract_rows(grad_scores, query) * scale
+
+
+def attend_specs(rows, length, head_dim, block):
+    by_rows = pl.BlockSpec((block, head_dim), lambda i: (i, 0))
+    by_row = pl.BlockSpec((block, 1), lambda i: (i, 0))
+    whole = pl.BlockSpec((length, head_dim), lambda i: (0, 0))
+    key_pos = pl.BlockSpec((1, length), lambda i: (0, 0))
+    return (rows // block,), by_rows, by_row, whole, key_pos
+
+
+def attend_cost(rows, length, head_dim, products):
+    return pl.CostEstimate(
+        flops=2 * products * rows * length * head_dim,
+        bytes_accessed=16 * rows * head_dim,
+        transcendentals=rows * length,
+    )
+
+
+def attend(query, key, value, query_pos, key_pos):
+    rows, head_dim = query.shape
+    length = key.shape[0]
+    grid, by_rows, by_row, whole, keys = attend_specs(rows, length, head_dim, 512)
+    return pl.pallas_call(
+        attend_kernel,
+        grid=grid,
+        in_specs=[by_rows, whole, whole, by_row, keys],
+        out_specs=[by_rows, by_rows, by_row],
+        out_shape=[
+            jax.ShapeDtypeStruct((rows, head_dim), jnp.float32),
+            jax.ShapeDtypeStruct((rows, head_dim), jnp.bfloat16),
+            jax.ShapeDtypeStruct((rows, 1), jnp.float32),
+        ],
+        cost_estimate=attend_cost(rows, length, head_dim, 2),
+        compiler_params=pltpu.CompilerParams(vmem_limit_bytes=40 * 1024 * 1024),
+    )(query, key, value, query_pos, key_pos)
+
+
+def attend_back(query, key, value, query_pos, key_pos, attended, log_total, grad):
+    rows, head_dim = query.shape
+    length = key.shape[0]
+    grid, by_rows, by_row, whole, keys = attend_specs(rows, length, head_dim, 512)
+    return pl.pallas_call(
+        attend_back_kernel,
+        grid=grid,
+        in_specs=[by_rows, whole, whole, by_row, keys, by_rows, by_row, by_rows],
+        out_specs=[by_rows, whole, whole],
+        out_shape=[
+            jax.ShapeDtypeStruct((rows, head_dim), jnp.float32),
+            jax.ShapeDtypeStruct((length, head_dim), jnp.float32),
+            jax.ShapeDtypeStruct((length, head_dim), jnp.float32),
+        ],
+        cost_estimate=attend_cost(rows, length, head_dim, 5),
+        compiler_params=pltpu.CompilerParams(vmem_limit_bytes=48 * 1024 * 1024),
+    )(query, key, value, query_pos, key_pos, attended, log_total, grad)
+
+
+def rotate_rows(values, cosine, sine):
+    half_dim = values.shape[-1] // 2
+    turned = jnp.concatenate([-values[:, half_dim:], values[:, :half_dim]], -1)
+    return values * cosine + turned * sine
+
+
+def split_shards(
+    tokens,
+    span_order,
+    w_query,
+    key_matrix,
+    value_matrix,
+    w_output,
+    w_gate,
+    w_up,
+    w_down,
+    norm_gains,
+    head_gains,
+    cotangent,
+):
+    low, wide = jnp.bfloat16, jnp.float32
+    dp_size, seq_size = lax.axis_size("dp"), lax.axis_size("seq")
+    row_count, width = tokens.shape
+    head_dim = head_gains.shape[1]
+    groups = w_query.shape[1] // key_matrix.shape[1]
+    pair_cols = groups * head_dim
+    qkv_cols = pair_cols + 2 * head_dim
+    unit_cols = w_gate.shape[1] // dp_size
+    weight_rows = w_query.shape[0]
+    length = seq_size * row_count
+    span_len = row_count // 2
+    seq_index = lax.axis_index("seq")
+
+    seq_tokens = gathered(tokens, "seq")
+    cotangent, tokens = lax.optimization_barrier((cotangent, tokens))
+
+    def cut(weight, parts):
+        return weight.reshape(weight_rows, parts, -1).transpose(1, 0, 2)
+
+    gain_cols = jnp.pad(norm_gains.T, ((0, 0), (0, 126)))
+    gain_cols = jnp.broadcast_to(gain_cols[None], (seq_size, weight_rows, 128))
+    first_part = [cut(w, seq_size) for w in (w_query, key_matrix, value_matrix, w_output.T)]
+    first_part = to_seq(jnp.concatenate(first_part + [gain_cols], -1))
+    first_part = first_part.reshape(seq_size * weight_rows, -1)
+    first_part = gather_dp(first_part)
+    team_cotangent = gather_team(cotangent)
+    first_part, w_gate, w_up, w_down = lax.optimization_barrier((first_part, w_gate, w_up, w_down))
+    second_part = jnp.concatenate([cut(w, dp_size) for w in (w_gate, w_up, w_down.T)], -1)
+    second_part = over_dp(second_part).reshape(dp_size * weight_rows, -1)
+    seq_tokens, second_part = lax.optimization_barrier((seq_tokens, second_part))
+    second_part = gathered(second_part, "seq").reshape(seq_size, dp_size, weight_rows, -1)
+    second_part = second_part.transpose(1, 0, 2, 3).reshape(width, -1)
+    w_gate_up = second_part[:, : 2 * unit_cols]
+    wd_turned = second_part[:, 2 * unit_cols :]
+    w_qkv = first_part[:, :qkv_cols]
+    wo_turned = first_part[:, qkv_cols : qkv_cols + pair_cols]
+    gains = first_part[:, qkv_cols + pair_cols :][:, :2].T.astype(wide)
+    offsets = jnp.arange(span_len, dtype=jnp.int32)
+    positions = (span_order[0][:, None] * span_len + offsets).reshape(length)
+    cosine, sine = rope_tables(positions, head_dim)
+    gains_head = head_gains.astype(wide)
+    inputs = tokens.astype(wide)
+    seq_inputs = seq_tokens.astype(wide)
+    inverse = lax.rsqrt(jnp.mean(seq_inputs * seq_inputs, axis=-1, keepdims=True) + eps_model)
+    seq_scaled = seq_inputs * inverse
+    normed_low = (seq_scaled * gains[0]).astype(low)
+    qkv_pre = jnp.dot(normed_low, w_qkv, preferred_element_type=wide)
+
+    def prepare(flat, gain):
+        return rotate_rows(rms_scale(flat, gain), cosine, sine)
+
+    def head_of(array, n):
+        return array[:, n * head_dim : (n + 1) * head_dim]
+
+    query_rot, query_back = [], []
+    for n in range(groups):
+        rotated, back = jax.vjp(prepare, head_of(qkv_pre, n), gains_head[0])
+        query_rot.append(rotated.astype(low))
+        query_back.append(back)
+    key_rot, key_back = jax.vjp(prepare, head_of(qkv_pre, groups), gains_head[1])
+    key_low = key_rot.astype(low)
+    value_low = head_of(qkv_pre, groups + 1).astype(low)
+    query_low = jnp.concatenate(query_rot, 0)
+
+    def heads_down(array):
+        return jnp.concatenate([head_of(array, n) for n in range(groups)], 0)
+
+    def heads_across(array):
+        return jnp.concatenate([array[n * length : (n + 1) * length] for n in range(groups)], 1)
+
+    query_pos = jnp.concatenate([positions] * groups)[:, None]
+    key_pos = positions[None, :]
+    attended, attended_low, log_total = attend(query_low, key_low, value_low, query_pos, key_pos)
+    attended_low = heads_across(attended_low)
+    middle = inputs + scatter_seq(contract_cols(attended_low, wo_turned))
+
+    normed_two, norm_two_back = jax.vjp(rms_scale, middle, gains[1])
+    normed_two_low = gather_team(normed_two.astype(low))
+    gate_up = jnp.dot(normed_two_low, w_gate_up, preferred_element_type=wide)
+    hidden, swiglu_back = jax.vjp(swiglu, gate_up[:, :unit_cols], gate_up[:, unit_cols:])
+    hidden_low = hidden.astype(low)
+    grad_hidden = jnp.dot(team_cotangent, wd_turned, preferred_element_type=wide)
+    grad_gate, grad_up = swiglu_back(grad_hidden)
+    gate_up_low = jnp.concatenate([grad_gate.astype(low), grad_up.astype(low)], -1)
+    partial = contract_cols(gate_up_low, w_gate_up)
+    partial, normed_two_low, gate_up_low = lax.optimization_barrier(
+        (partial, normed_two_low, gate_up_low)
+    )
+    second_grads = jnp.concatenate(
+        [contract_rows(normed_two_low, gate_up_low), contract_rows(team_cotangent, hidden_low)], -1
+    ).astype(low)
+    second_grads = second_grads.reshape(dp_size, seq_size, weight_rows, -1)
+    second_grads = second_grads.transpose(1, 0, 2, 3).reshape(width, -1)
+    partial = scatter_step(partial, 1)
+    partial, second_grads = lax.optimization_barrier((partial, second_grads))
+    second_grads = summed(second_grads, "seq")
+    grad_middle_norm, grad_gain_two = norm_two_back(scatter_rest(partial))
+    grad_middle = cotangent.astype(wide) + grad_middle_norm
+    middle_low = gather_seq(grad_middle.astype(low))
+    out_partial = contract_cols(hidden_low, wd_turned)
+    out_partial, middle_low = lax.optimization_barrier((out_partial, middle_low))
+    out_partial = scatter_step(out_partial, 1)
+
+    grad_att = jnp.dot(middle_low, wo_turned, preferred_element_type=wide).astype(low)
+    grad_att, out_partial = lax.optimization_barrier((grad_att, out_partial))
+    output = middle + scatter_rest(out_partial)
+    grad_query, grad_key, grad_value = attend_back(
+        query_low,
+        key_low,
+        value_low,
+        query_pos,
+        key_pos,
+        attended,
+        log_total,
+        heads_down(grad_att),
+    )
+    grad_query, grad_key, grad_value, output = lax.optimization_barrier(
+        (grad_query, grad_key, grad_value, output)
+    )
+    grad_qkv, gain_query = [], 0.0
+    for n in range(groups):
+        before, gain = query_back[n](grad_query[n * length : (n + 1) * length])
+        grad_qkv.append(before.astype(low))
+        gain_query = gain_query + gain
+    before, gain_key = key_back(grad_key)
+    grad_qkv = jnp.concatenate(grad_qkv + [before.astype(low), grad_value.astype(low)], -1)
+    partial = contract_cols(grad_qkv, w_qkv)
+    grad_gain_one = jnp.sum(partial * seq_scaled, axis=0)
+    def in_columns(cols):
+        return jnp.pad(cols, ((0, 0), (0, 128 - cols.shape[1])))
+
+    seq_rows = seq_size * weight_rows
+    head_gain = jnp.stack([gain_query, gain_key], 1)
+    head_gain = jnp.pad(head_gain, ((0, seq_rows - head_dim), (0, 0)))
+    head_gain = jnp.concatenate([head_gain] * dp_size, 0)
+    gain_cols = jnp.concatenate([jnp.stack([grad_gain_one, grad_gain_two], 1), head_gain], 1)
+    first_grads = jnp.concatenate(
+        [
+            contract_rows(normed_low, grad_qkv).astype(low),
+            contract_rows(middle_low, attended_low).astype(low),
+            in_columns(gain_cols).astype(low),
+        ],
+        1,
+    )
+    first_grads, partial = lax.optimization_barrier((first_grads, partial))
+    bit = dp_size // 2
+    while bit:
+        first_grads = sum_row_halves(first_grads, "dp", bit)
+        bit //= 2
+    grad_normed = scatter_seq(partial)
+    grad_normed, first_grads, second_grads = lax.optimization_barrier(
+        (grad_normed, first_grads.astype(low), second_grads)
+    )
+    _, norm_back = jax.vjp(lambda values: rms_scale(values, gains[0]), inputs)
+    grad_input = grad_middle + norm_back(grad_normed)[0]
+
+    matrix_cols = qkv_cols + pair_cols
+    gain_cols = first_grads[:, matrix_cols:]
+    head_gain = gain_cols[:head_dim, 2:4].reshape(weight_rows, -1)
+    head_width = head_gain.shape[1]
+    head_gain = jnp.concatenate([head_gain] * seq_size, 0)
+    gain_cols = in_columns(jnp.concatenate([gain_cols[:, :2], head_gain], 1))
+    first_grads = jnp.concatenate([first_grads[:, :matrix_cols], gain_cols], 1)
+    first_grads = to_seq(first_grads.reshape(seq_size, weight_rows, -1))
+    gain_cols = jnp.sum(first_grads[..., matrix_cols:].astype(wide), 0)
+    grad_norm = gain_cols[:, :2].T
+    grad_head = gain_cols[:, 2 : 2 + head_width].reshape(head_dim, 2).T
+
+    second_grads = over_dp(second_grads.reshape(dp_size, weight_rows, -1))
+
+    def joined(blocks, start, cols):
+        parts = [blocks[n, :, start : start + cols] for n in range(blocks.shape[0])]
+        return jnp.concatenate(parts, 1).astype(wide)
+
+    return (
+        output.astype(low),
+        grad_input.astype(low),
+        joined(first_grads, 0, pair_cols),
+        joined(first_grads, pair_cols, head_dim),
+        joined(first_grads, pair_cols + head_dim, head_dim),
+        joined(first_grads, qkv_cols, pair_cols).T,
+        joined(second_grads, 0, unit_cols),
+        joined(second_grads, unit_cols, unit_cols),
+        joined(second_grads, 2 * unit_cols, unit_cols).T,
+        grad_norm,
+        grad_head,
+    )
+
+
 def solution(mesh):
+    sizes = dict(mesh.shape)
+
+    def layer(*arrays):
+        query_cols, key_cols = arrays[2].shape[1], arrays[3].shape[1]
+        kv_heads = key_cols // arrays[10].shape[1]
+        dp, seq = sizes["dp"], sizes["seq"]
+        fits = dp > 1 and dp & (dp - 1) == 0 and seq & (seq - 1) == 0 and kv_heads == seq
+        fits = fits and arrays[6].shape[1] % (128 * dp) == 0
+        return mapped(split_shards if fits else shards, mesh)(*arrays)
+
+    return layer
+
+
+def mapped(function, mesh):
     return jax.shard_map(
-        shards,
+        function,
         mesh=mesh,
         in_specs=(
             P(("dp", "seq"), None),

time: 2200 us -> 406 us (0.18)
  waiting for transfers between devices: 1750 us -> 167 us
  blocking collectives: 132 us -> 28.6 us
  matrix products: 113 us -> 18.5 us
  starting transfers between devices: 36.7 us -> 82.7 us
  other arithmetic: 72.5 us -> 41 us
  local copies, waits for them, and re-layouts: 62.3 us -> 36.4 us
    reduce_scatter x6 -> x1, waiting for transfers between devices: 980 us -> 0.02 us  [summed(): return lax.psum_scatter(array, axis, scatter_dimension=0, tiled=True)]
    all_gather x9 -> x2, waiting for transfers between devices: 417 us -> 0.01 us  [gathered(): return lax.all_gather(array, axis, axis=0, tiled=True)]
    unnamed x19 -> x3, waiting for transfers between devices: 203 us -> 0.71 us
    all_gather x1 -> x0, blocking collectives: 69.5 us -> none  [shards(): lax.all_gather(norm_gains, ('dp', 'seq'), axis=1, tiled=True)]
    psum x1 -> x0, blocking collectives: 63 us -> none  [shards(): lax.psum(jnp.stack([grad_gain_query, grad_gain_key]), ('dp', 'seq'))]
    dot_general x51 -> x4, matrix products: 59.7 us -> 5.39 us  [the longest x1 1.8 us: split_shards(): gate_up = jnp.dot(normed_two_low, w_gate_up, preferred_element_type=wide)]
    ppermute x24 -> x33, starting transfers between devices: 35.3 us -> 69.4 us  [swapped(): lax.ppermute(array, axis, [(i, i ^ by) for i in range(lax.axis_size(axis))])]
    dot_general x7 -> x4, matrix products: 34 us -> 5.04 us  [contract_rows(): lax.dot_general(left, right, (((0,), (0,)), ((), ())), preferred_element_...]
  transfers between devices with their start and end apart: 41 -> 39, of which waited for: 40 -> 23; matrix products, arithmetic and copies ran while one was open for 6% -> 17% of each run, Pallas kernels for 0% -> 4%
where the time goes in v2:
time: 406 us; the launch traced here: 405 us
  waiting for transfers between devices  167 us (41%)
  starting transfers between devices  82.7 us (20%)
  other arithmetic  41 us (10%)
  local copies, waits for them, and re-layouts  36.4 us (9%)
  blocking collectives  28.6 us (7%)
  matrix products  18.5 us (5%)
  Pallas kernels  15.6 us (4%)
  between operations  15.2 us (4%)
    ppermute x33, waiting for transfers between devices, swapped(): lax.ppermute(array, axis, [(i, i ^ by) for i in range(lax.axis_size(axis))])  138 us
    ppermute x33, starting transfers between devices, swapped(): lax.ppermute(array, axis, [(i, i ^ by) for i in range(lax.axis_size(axis))])  69.4 us
    all_to_all x1, blocking collectives, to_seq(): return lax.all_to_all(array, 'seq', 0, 0, tiled=True)  28.6 us
    all_to_all x2, waiting for transfers between devices, over_dp(): return lax.all_to_all(array, 'dp', 0, 0, tiled=True)  17.9 us
    unnamed x117, local copies, waits for them, and re-layouts  17.7 us
    all_to_all x1, waiting for transfers between devices, to_seq(): return lax.all_to_all(array, 'seq', 0, 0, tiled=True)  10.6 us
    pallas_call x1, Pallas kernels, attend_back(): pl.pallas_call(attend_back_kernel, grid=grid, in_specs=[by_rows, whole, w...  8.58 us
    convert_element_type x6, other arithmetic, scatter_seq(): sums.append(pair.astype(low) if n else pair)  8.36 us
  transfers between devices with their start and end apart: 39, of which 23 were waited for; matrix products, arithmetic and copies ran while one was open for 17% of the time, Pallas kernels for 4%

profile of v2, /device:TPU:0, one launch (start us, length us, event | category | flops | bytes accessed | tf_op | source)
XLA Modules:
  0.0 404.9 jit_solution(5881759647036780936)
XLA Ops:
  12.5 28.6 %all_to_all.20 = bf16[8,32,896]{2,1,0:T(8,128)(2,1)S(1)} all-to-all(bf16[8,32,896]{2,1,0:T(8,128)(2,1)S(1)} %copy.84), channel_id=1, replica_groups=mesh['dp'=4,'seq'=8] {'seq'}, dimensions={0} | all-to-all | bytes 917504 | tf_op jit(solution)/shard_map/all_to_all | solution.py:475
  42.6 7.0 %collective-permute-done = bf16[256,896]{1,0:T(8,128)(2,1)S(1)} collective-permute-done((bf16[256,896]{1,0:T(8,128)(2,1)S(1)}, bf16[256,896]{1,0:T(8,128)(2,1)S(1)}, u32[]{:S(2)}, u32[]{:S(2)}) %collective-permute-start) | collective-permute-done | bytes 458784 | tf_op jit(solution)/shard_map/ppermute | solution.py:375
  62.8 9.3 %all-to-all-done.1 = bf16[4,32,2304]{2,1,0:T(8,128)(2,1)S(1)} async-done(((bf16[4,32,2304]{2,1,0:T(8,128)(2,1)}), bf16[4,32,2304]{2,1,0:T(8,128)(2,1)S(1)}, u32[]{:S(2)}, u32[]{:S(2)}) %all-to-all-start.1) | async-done | bytes 589856 | tf_op jit(solution)/shard_map/all_to_all | solution.py:379
  82.4 7.0 %shard_map.203 = (f32[2048,128]{1,0:T(8,128)S(1)}, bf16[2048,128]{1,0:T(8,128)(2,1)S(1)}, f32[2048,1]{1,0:T(8,128)S(1)}) custom-call(bf16[2048,128]{1,0:T(8,128)(2,1)S(1)} %pad_maximum_fusion.9.query_ref, bf16[1024,128]{1,0:T(8,128)(2,1)S(1)} %get-tuple-element.184.key_ref, bf16[1024,128]{1,0:T(8,128)(2,1)S(1)} %slice.607.value_ref, ...), custom_call_target="tpu_custom_call" | custom-call | flops 1073741824 | bytes 4194304 | tf_op jit(solution)/shard_map/pallas_call | solution.py:544
  97.6 6.0 %collective-permute-done.5 = bf16[128,1024]{1,0:T(8,128)(2,1)} collective-permute-done((bf16[128,1024]{1,0:T(8,128)(2,1)}, bf16[128,1024]{1,0:T(8,128)(2,1)}, u32[]{:S(2)}, u32[]{:S(2)}) %collective-permute-start.5) | collective-permute-done | bytes 262176 | tf_op jit(solution)/shard_map/ppermute | solution.py:375
  117.5 7.2 %collective-permute-done.6 = bf16[128,1024]{1,0:T(8,128)(2,1)} collective-permute-done((bf16[128,1024]{1,0:T(8,128)(2,1)}, bf16[128,1024]{1,0:T(8,128)(2,1)}, u32[]{:S(2)}, u32[]{:S(2)}) %collective-permute-start.6) | collective-permute-done | bytes 262176 | tf_op jit(solution)/shard_map/ppermute | solution.py:375
  124.7 21.4 %collective-permute-start.7 = (bf16[128,1024]{1,0:T(8,128)(2,1)}, bf16[128,1024]{1,0:T(8,128)(2,1)}, u32[]{:S(2)}, u32[]{:S(2)}) collective-permute-start(bf16[128,1024]{1,0:T(8,128)(2,1)} %add_convert_fusion.5), channel_id=1, source_target_pairs={{0,4},{1,5},{2,6},{3,7},{4,0},{5,1},{6,2},{7,3},{8,12},{9,13},{10,... | collective-permute-start | bytes 786440 | tf_op jit(solution)/shard_map/ppermute | solution.py:375
  148.0 14.3 %collective-permute-done.7 = bf16[128,1024]{1,0:T(8,128)(2,1)} collective-permute-done((bf16[128,1024]{1,0:T(8,128)(2,1)}, bf16[128,1024]{1,0:T(8,128)(2,1)}, u32[]{:S(2)}, u32[]{:S(2)}) %collective-permute-start.7) | collective-permute-done | bytes 262176 | tf_op jit(solution)/shard_map/ppermute | solution.py:375
  162.7 11.0 %collective-permute-done.8 = bf16[128,1024]{1,0:T(8,128)(2,1)} collective-permute-done((bf16[128,1024]{1,0:T(8,128)(2,1)}, bf16[128,1024]{1,0:T(8,128)(2,1)}, u32[]{:S(2)}, u32[]{:S(2)}) %collective-permute-start.8) | collective-permute-done | bytes 262176 | tf_op jit(solution)/shard_map/ppermute | solution.py:375
  177.6 5.0 %collective-permute-done.9 = bf16[128,1024]{1,0:T(8,128)(2,1)S(1)} collective-permute-done((bf16[128,1024]{1,0:T(8,128)(2,1)S(1)}, bf16[128,1024]{1,0:T(8,128)(2,1)S(1)}, u32[]{:S(2)}, u32[]{:S(2)}) %collective-permute-start.9) | collective-permute-done | bytes 262176 | tf_op jit(solution)/shard_map/ppermute | solution.py:375
  205.8 8.0 %collective-permute-done.14 = bf16[128,1024]{1,0:T(8,128)(2,1)} collective-permute-done((bf16[128,1024]{1,0:T(8,128)(2,1)}, bf16[128,1024]{1,0:T(8,128)(2,1)}, u32[]{:S(2)}, u32[]{:S(2)}) %collective-permute-start.14) | collective-permute-done | bytes 262176 | tf_op jit(solution)/shard_map/ppermute | solution.py:375
  224.1 20.6 %collective-permute-done.16 = bf16[128,1024]{1,0:T(8,128)(2,1)} collective-permute-done((bf16[128,1024]{1,0:T(8,128)(2,1)}, bf16[128,1024]{1,0:T(8,128)(2,1)}, u32[]{:S(2)}, u32[]{:S(2)}) %collective-permute-start.16) | collective-permute-done | bytes 262176 | tf_op jit(solution)/shard_map/ppermute | solution.py:375
  250.8 5.4 %collective-permute-done.20 = bf16[128,1024]{1,0:T(8,128)(2,1)S(1)} collective-permute-done((bf16[128,1024]{1,0:T(8,128)(2,1)}, bf16[128,1024]{1,0:T(8,128)(2,1)S(1)}, u32[]{:S(2)}, u32[]{:S(2)}) %collective-permute-start.20) | collective-permute-done | bytes 262176 | tf_op jit(solution)/shard_map/ppermute | solution.py:375
  270.0 8.6 %shard_map.204 = (f32[2048,128]{1,0:T(8,128)S(1)}, f32[1024,128]{1,0:T(8,128)S(1)}, f32[1024,128]{1,0:T(8,128)S(1)}) custom-call(bf16[2048,128]{1,0:T(8,128)(2,1)S(1)} %pad_maximum_fusion.9.query_ref, bf16[1024,128]{1,0:T(8,128)(2,1)S(1)} %get-tuple-element.184.key_ref, bf16[1024,128]{1,0:T(8,128)(2,1)S(1)} %slice.607.value_ref, ...), custom_call_target="tpu_custom_call" | custom-call | flops 2684354560 | bytes 4194304 | tf_op jit(solution)/shard_map/pallas_call | solution.py:563
  291.2 7.1 %collective-permute-done.27 = bf16[128,1024]{1,0:T(8,128)(2,1)S(1)} collective-permute-done((bf16[128,1024]{1,0:T(8,128)(2,1)S(1)}, bf16[128,1024]{1,0:T(8,128)(2,1)S(1)}, u32[]{:S(2)}, u32[]{:S(2)}) %collective-permute-start.27) | collective-permute-done | bytes 262176 | tf_op jit(solution)/shard_map/ppermute | solution.py:375
  298.3 5.6 %collective-permute-done.26 = bf16[128,1024]{1,0:T(8,128)(2,1)S(1)} collective-permute-done((bf16[128,1024]{1,0:T(8,128)(2,1)S(1)}, bf16[128,1024]{1,0:T(8,128)(2,1)S(1)}, u32[]{:S(2)}, u32[]{:S(2)}) %collective-permute-start.26) | collective-permute-done | bytes 262176 | tf_op jit(solution)/shard_map/ppermute | solution.py:375
  307.2 4.7 %collective-permute-done.25 = bf16[128,1024]{1,0:T(8,128)(2,1)S(1)} collective-permute-done((bf16[128,1024]{1,0:T(8,128)(2,1)S(1)}, bf16[128,1024]{1,0:T(8,128)(2,1)S(1)}, u32[]{:S(2)}, u32[]{:S(2)}) %collective-permute-start.25) | collective-permute-done | bytes 262176 | tf_op jit(solution)/shard_map/ppermute | solution.py:375
  312.5 6.0 %collective-permute-done.28 = bf16[128,1024]{1,0:T(8,128)(2,1)} collective-permute-done((bf16[128,1024]{1,0:T(8,128)(2,1)S(1)}, bf16[128,1024]{1,0:T(8,128)(2,1)}, u32[]{:S(2)}, u32[]{:S(2)}) %collective-permute-start.28) | collective-permute-done | bytes 262176 | tf_op jit(solution)/shard_map/ppermute | solution.py:375
  318.5 19.0 %collective-permute-start.29 = (bf16[128,1024]{1,0:T(8,128)(2,1)}, bf16[128,1024]{1,0:T(8,128)(2,1)}, u32[]{:S(2)}, u32[]{:S(2)}) collective-permute-start(bf16[128,1024]{1,0:T(8,128)(2,1)} %add_convert_fusion.2), channel_id=1, source_target_pairs={{0,4},{1,5},{2,6},{3,7},{4,0},{5,1},{6,2},{7,3},{8,12},{9,13},{10,... | collective-permute-start | bytes 786440 | tf_op jit(solution)/shard_map/ppermute | solution.py:375
  339.4 10.3 %collective-permute-done.29 = bf16[128,1024]{1,0:T(8,128)(2,1)} collective-permute-done((bf16[128,1024]{1,0:T(8,128)(2,1)}, bf16[128,1024]{1,0:T(8,128)(2,1)}, u32[]{:S(2)}, u32[]{:S(2)}) %collective-permute-start.29) | collective-permute-done | bytes 262176 | tf_op jit(solution)/shard_map/ppermute | solution.py:375
  352.6 4.8 %collective-permute-done.30 = bf16[128,1024]{1,0:T(8,128)(2,1)S(1)} collective-permute-done((bf16[128,1024]{1,0:T(8,128)(2,1)}, bf16[128,1024]{1,0:T(8,128)(2,1)S(1)}, u32[]{:S(2)}, u32[]{:S(2)}) %collective-permute-start.30) | collective-permute-done | bytes 262176 | tf_op jit(solution)/shard_map/ppermute | solution.py:375
  366.1 8.6 %all-to-all-done.3 = bf16[4,32,2304]{2,1,0:T(8,128)(2,1)S(1)} async-done(((bf16[4,32,2304]{2,1,0:T(8,128)(2,1)}), bf16[4,32,2304]{2,1,0:T(8,128)(2,1)S(1)}, u32[]{:S(2)}, u32[]{:S(2)}) %all-to-all-start.3) | async-done | bytes 589856 | tf_op jit(solution)/shard_map/all_to_all | solution.py:379
  374.7 6.3 %all-to-all-start.2 = ((bf16[8,32,896]{2,1,0:T(8,128)(2,1)}), bf16[8,32,896]{2,1,0:T(8,128)(2,1)S(1)}, u32[]{:S(2)}, u32[]{:S(2)}) async-start(bf16[8,32,896]{2,1,0:T(8,128)(2,1)} %bitcast.29), calls=%async_computation.3 | async-start | bytes 917504 | tf_op jit(solution)/shard_map/all_to_all | solution.py:475
  383.4 10.6 %all-to-all-done.2 = bf16[8,32,896]{2,1,0:T(8,128)(2,1)S(1)} async-done(((bf16[8,32,896]{2,1,0:T(8,128)(2,1)}), bf16[8,32,896]{2,1,0:T(8,128)(2,1)S(1)}, u32[]{:S(2)}, u32[]{:S(2)}) %all-to-all-start.2) | async-done | bytes 458784 | tf_op jit(solution)/shard_map/all_to_all | solution.py:475
  (322 shorter events, 147.6 us)
Async XLA Ops:
  7.2 65.0 %all-gather.3.cloned.1.call-start = ((), (), s32[]{:S(2)}) async-start(), calls=%async_computation.5 | async-start | bytes 2359296 | tf_op jit(solution)/shard_map/all_gather | solution.py:383
  59.1 13.0 %all-to-all-start.1 = ((bf16[4,32,2304]{2,1,0:T(8,128)(2,1)}), bf16[4,32,2304]{2,1,0:T(8,128)(2,1)S(1)}, u32[]{:S(2)}, u32[]{:S(2)}) async-start(bf16[4,32,2304]{2,1,0:T(8,128)(2,1)} %copy.89), calls=%async_computation.1 | async-start | bytes 1179648 | tf_op jit(solution)/shard_map/all_to_all | solution.py:379
  62.6 124.0 %all-gather.5.cloned.1.call-start = ((), (), s32[]{:S(2)}) async-start(), calls=%async_computation.6 | async-start | bytes 5308416 | tf_op jit(solution)/shard_map/all_gather | solution.py:383
  73.0 287.0 %reduce-scatter.2.cloned.1.call-start = ((), (), s32[]{:S(2)}) async-start(), calls=%async_computation.7 | async-start | bytes 5308416 | tf_op jit(solution)/shard_map/reduce_scatter | solution.py:387
  95.6 13.7 %collective-permute-start.4 = (bf16[128,1024]{1,0:T(8,128)(2,1)}, bf16[128,1024]{1,0:T(8,128)(2,1)}, u32[]{:S(2)}, u32[]{:S(2)}) collective-permute-start(bf16[128,1024]{1,0:T(8,128)(2,1)} %get-tuple-element.172), channel_id=1, source_target_pairs={{0,1},{1,0},{2,3},{3,2},{4,5},{5,4},{6,7},{7,6},{8,9},{9,8},{10,11... | collective-permute-start | bytes 786440 | tf_op jit(solution)/shard_map/ppermute | solution.py:375
  96.2 21.3 %collective-permute-start.3 = (bf16[128,1024]{1,0:T(8,128)(2,1)}, bf16[128,1024]{1,0:T(8,128)(2,1)}, u32[]{:S(2)}, u32[]{:S(2)}) collective-permute-start(bf16[128,1024]{1,0:T(8,128)(2,1)} %get-tuple-element.173), channel_id=1, source_target_pairs={{0,1},{1,0},{2,3},{3,2},{4,5},{5,4},{6,7},{7,6},{8,9},{9,8},{10,11... | collective-permute-start | bytes 786440 | tf_op jit(solution)/shard_map/ppermute | solution.py:375
  109.3 15.4 %collective-permute-start.6 = (bf16[128,1024]{1,0:T(8,128)(2,1)}, bf16[128,1024]{1,0:T(8,128)(2,1)}, u32[]{:S(2)}, u32[]{:S(2)}) collective-permute-start(bf16[128,1024]{1,0:T(8,128)(2,1)} %add_convert_fusion.6), channel_id=1, source_target_pairs={{0,6},{1,7},{2,4},{3,5},{4,2},{5,3},{6,0},{7,1},{8,14},{9,15},{10,... | collective-permute-start | bytes 786440 | tf_op jit(solution)/shard_map/ppermute | solution.py:375
  113.1 34.9 %collective-permute-start.2 = (bf16[128,1024]{1,0:T(8,128)(2,1)}, bf16[128,1024]{1,0:T(8,128)(2,1)}, u32[]{:S(2)}, u32[]{:S(2)}) collective-permute-start(bf16[128,1024]{1,0:T(8,128)(2,1)} %get-tuple-element.174), channel_id=1, source_target_pairs={{0,1},{1,0},{2,3},{3,2},{4,5},{5,4},{6,7},{7,6},{8,9},{9,8},{10,11... | collective-permute-start | bytes 786440 | tf_op jit(solution)/shard_map/ppermute | solution.py:375
  124.7 37.6 %collective-permute-start.7 = (bf16[128,1024]{1,0:T(8,128)(2,1)}, bf16[128,1024]{1,0:T(8,128)(2,1)}, u32[]{:S(2)}, u32[]{:S(2)}) collective-permute-start(bf16[128,1024]{1,0:T(8,128)(2,1)} %add_convert_fusion.5), channel_id=1, source_target_pairs={{0,4},{1,5},{2,6},{3,7},{4,0},{5,1},{6,2},{7,3},{8,12},{9,13},{10,... | collective-permute-start | bytes 786440 | tf_op jit(solution)/shard_map/ppermute | solution.py:375
  162.3 14.3 %collective-permute-start.11 = (bf16[128,1024]{1,0:T(8,128)(2,1)}, bf16[128,1024]{1,0:T(8,128)(2,1)}, u32[]{:S(2)}, u32[]{:S(2)}) collective-permute-start(bf16[128,1024]{1,0:T(8,128)(2,1)} %param.23), channel_id=1, source_target_pairs={{0,16},{8,24},{16,0},{24,8},{1,17},{9,25},{17,1},{25,9},{2,18},{10... | collective-permute-start | bytes 786440 | tf_op jit(solution)/shard_map/ppermute | solution.py:375
  218.9 25.7 %collective-permute-start.16 = (bf16[128,1024]{1,0:T(8,128)(2,1)}, bf16[128,1024]{1,0:T(8,128)(2,1)}, u32[]{:S(2)}, u32[]{:S(2)}) collective-permute-start(bf16[128,1024]{1,0:T(8,128)(2,1)} %get-tuple-element.161), channel_id=1, source_target_pairs={{0,2},{1,3},{2,0},{3,1},{4,6},{5,7},{6,4},{7,5},{8,10},{9,11},{10,... | collective-permute-start | bytes 786440 | tf_op jit(solution)/shard_map/ppermute | solution.py:375
  218.9 30.7 %collective-permute-start.15 = (bf16[128,1024]{1,0:T(8,128)(2,1)}, bf16[128,1024]{1,0:T(8,128)(2,1)S(1)}, u32[]{:S(2)}, u32[]{:S(2)}) collective-permute-start(bf16[128,1024]{1,0:T(8,128)(2,1)} %get-tuple-element.161), channel_id=1, source_target_pairs={{0,1},{1,0},{2,3},{3,2},{4,5},{5,4},{6,7},{7,6},{8,9},{9,8},{10,11... | collective-permute-start | bytes 786440 | tf_op jit(solution)/shard_map/ppermute | solution.py:375
  219.7 28.5 %collective-permute-start.18 = (bf16[128,1024]{1,0:T(8,128)(2,1)}, bf16[128,1024]{1,0:T(8,128)(2,1)S(1)}, u32[]{:S(2)}, u32[]{:S(2)}) collective-permute-start(bf16[128,1024]{1,0:T(8,128)(2,1)} %get-tuple-element.161), channel_id=1, source_target_pairs={{0,4},{1,5},{2,6},{3,7},{4,0},{5,1},{6,2},{7,3},{8,12},{9,13},{10,... | collective-permute-start | bytes 786440 | tf_op jit(solution)/shard_map/ppermute | solution.py:375
  222.3 33.9 %collective-permute-start.20 = (bf16[128,1024]{1,0:T(8,128)(2,1)}, bf16[128,1024]{1,0:T(8,128)(2,1)S(1)}, u32[]{:S(2)}, u32[]{:S(2)}) collective-permute-start(bf16[128,1024]{1,0:T(8,128)(2,1)} %get-tuple-element.161), channel_id=1, source_target_pairs={{0,6},{1,7},{2,4},{3,5},{4,2},{5,3},{6,0},{7,1},{8,14},{9,15},{10,... | collective-permute-start | bytes 786440 | tf_op jit(solution)/shard_map/ppermute | solution.py:375
  244.7 12.3 %collective-permute-start.17 = (bf16[128,1024]{1,0:T(8,128)(2,1)}, bf16[128,1024]{1,0:T(8,128)(2,1)S(1)}, u32[]{:S(2)}, u32[]{:S(2)}) collective-permute-start(bf16[128,1024]{1,0:T(8,128)(2,1)} %collective-permute-done.16), channel_id=1, source_target_pairs={{0,1},{1,0},{2,3},{3,2},{4,5},{5,4},{6,7},{7,6},{8,9},{9,8},{10,11... | collective-permute-start | bytes 786440 | tf_op jit(solution)/shard_map/ppermute | solution.py:375
  248.1 13.2 %collective-permute-start.19 = (bf16[128,1024]{1,0:T(8,128)(2,1)S(1)}, bf16[128,1024]{1,0:T(8,128)(2,1)S(1)}, u32[]{:S(2)}, u32[]{:S(2)}) collective-permute-start(bf16[128,1024]{1,0:T(8,128)(2,1)S(1)} %collective-permute-done.18), channel_id=1, source_target_pairs={{0,1},{1,0},{2,3},{3,2},{4,5},{5,4},{6,7},{7,6},{8,9},{9,8},{10,11... | collective-permute-start | bytes 786440 | tf_op jit(solution)/shard_map/ppermute | solution.py:375
  288.9 60.8 %collective-permute-start.31 = (bf16[512,896]{0,1:T(8,128)(2,1)S(1)}, bf16[512,896]{0,1:T(8,128)(2,1)}, u32[]{:S(2)}, u32[]{:S(2)}) collective-permute-start(bf16[512,896]{0,1:T(8,128)(2,1)S(1)} %constant_dynamic-slice_fusion), channel_id=1, source_target_pairs={{0,16},{8,24},{16,0},{24,8},{1,17},{9,25},{17,1},{25,9},{2,18},{10... | collective-permute-start | bytes 2752520 | tf_op jit(solution)/shard_map/ppermute | solution.py:375
  289.1 14.7 %collective-permute-start.26 = (bf16[128,1024]{1,0:T(8,128)(2,1)S(1)}, bf16[128,1024]{1,0:T(8,128)(2,1)S(1)}, u32[]{:S(2)}, u32[]{:S(2)}) collective-permute-start(bf16[128,1024]{1,0:T(8,128)(2,1)S(1)} %get-tuple-element.168), channel_id=1, source_target_pairs={{0,1},{1,0},{2,3},{3,2},{4,5},{5,4},{6,7},{7,6},{8,9},{9,8},{10,11... | collective-permute-start | bytes 786440 | tf_op jit(solution)/shard_map/ppermute | solution.py:375
  291.1 20.7 %collective-permute-start.25 = (bf16[128,1024]{1,0:T(8,128)(2,1)S(1)}, bf16[128,1024]{1,0:T(8,128)(2,1)S(1)}, u32[]{:S(2)}, u32[]{:S(2)}) collective-permute-start(bf16[128,1024]{1,0:T(8,128)(2,1)S(1)} %get-tuple-element.169), channel_id=1, source_target_pairs={{0,1},{1,0},{2,3},{3,2},{4,5},{5,4},{6,7},{7,6},{8,9},{9,8},{10,11... | collective-permute-start | bytes 786440 | tf_op jit(solution)/shard_map/ppermute | solution.py:375
  303.8 14.7 %collective-permute-start.28 = (bf16[128,1024]{1,0:T(8,128)(2,1)S(1)}, bf16[128,1024]{1,0:T(8,128)(2,1)}, u32[]{:S(2)}, u32[]{:S(2)}) collective-permute-start(bf16[128,1024]{1,0:T(8,128)(2,1)S(1)} %add_convert_fusion.3), channel_id=1, source_target_pairs={{0,6},{1,7},{2,4},{3,5},{4,2},{5,3},{6,0},{7,1},{8,14},{9,15},{10,... | collective-permute-start | bytes 786440 | tf_op jit(solution)/shard_map/ppermute | solution.py:375
  305.5 33.9 %collective-permute-start.24 = (bf16[128,1024]{1,0:T(8,128)(2,1)S(1)}, bf16[128,1024]{1,0:T(8,128)(2,1)}, u32[]{:S(2)}, u32[]{:S(2)}) collective-permute-start(bf16[128,1024]{1,0:T(8,128)(2,1)S(1)} %get-tuple-element.170), channel_id=1, source_target_pairs={{0,1},{1,0},{2,3},{3,2},{4,5},{5,4},{6,7},{7,6},{8,9},{9,8},{10,11... | collective-permute-start | bytes 786440 | tf_op jit(solution)/shard_map/ppermute | solution.py:375
  318.5 31.2 %collective-permute-start.29 = (bf16[128,1024]{1,0:T(8,128)(2,1)}, bf16[128,1024]{1,0:T(8,128)(2,1)}, u32[]{:S(2)}, u32[]{:S(2)}) collective-permute-start(bf16[128,1024]{1,0:T(8,128)(2,1)} %add_convert_fusion.2), channel_id=1, source_target_pairs={{0,4},{1,5},{2,6},{3,7},{4,0},{5,1},{6,2},{7,3},{8,12},{9,13},{10,... | collective-permute-start | bytes 786440 | tf_op jit(solution)/shard_map/ppermute | solution.py:375
  361.7 13.0 %all-to-all-start.3 = ((bf16[4,32,2304]{2,1,0:T(8,128)(2,1)}), bf16[4,32,2304]{2,1,0:T(8,128)(2,1)S(1)}, u32[]{:S(2)}, u32[]{:S(2)}) async-start(bf16[4,32,2304]{2,1,0:T(8,128)(2,1)} %bitcast.63), calls=%async_computation.4 | async-start | bytes 1179648 | tf_op jit(solution)/shard_map/all_to_all | solution.py:379
  374.7 19.2 %all-to-all-start.2 = ((bf16[8,32,896]{2,1,0:T(8,128)(2,1)}), bf16[8,32,896]{2,1,0:T(8,128)(2,1)S(1)}, u32[]{:S(2)}, u32[]{:S(2)}) async-start(bf16[8,32,896]{2,1,0:T(8,128)(2,1)} %bitcast.29), calls=%async_computation.3 | async-start | bytes 917504 | tf_op jit(solution)/shard_map/all_to_all | solution.py:475
  (60 other events, 516.4 us)
Sparse Core Ops, SparseCore 0:
  10.1 57.8 all-gather.2
  73.1 98.0 all-gather.4
  205.9 129.3 reduce-scatter.1

commit v3 on v2

--- a/solution.py
+++ b/solution.py
@@ -1,3 +1,4 @@
+import functools
 import math
 
 import jax
@@ -387,21 +388,18 @@
     return lax.psum_scatter(array, axis, scatter_dimension=0, tiled=True)
 
 
-def gather_seq(rows):
-    count, place = lax.axis_size("seq"), lax.axis_index("seq")
-    row_count = rows.shape[0]
-    blocks = [rows, None]
-    for n in range(2, count, 2):
-        blocks += [swapped(rows, "seq", n), None]
-    for n in range(0, count, 2):
-        blocks[n + 1] = swapped(blocks[n], "seq", 1)
-    held = jnp.zeros((count * row_count,) + rows.shape[1:], rows.dtype)
-    for n, block in enumerate(blocks):
-        held = lax.dynamic_update_slice_in_dim(held, block, (place ^ n) * row_count, 0)
-    return held
-
-
-def scatter_seq(partial):
+def gather_seq(rows, later=None):
+    count = lax.axis_size("seq")
+    upper = [rows] + [swapped(rows, "seq", n) for n in range(2, count, 2)]
+    if later is not None:
+        *upper, later = lax.optimization_barrier((*upper, later))
+    blocks = []
+    for block in upper:
+        blocks += [block, swapped(block, "seq", 1)]
+    return blocks if later is None else (blocks, later)
+
+
+def scatter_seq(partial, later=()):
     low, wide = jnp.bfloat16, jnp.float32
     count, place = lax.axis_size("seq"), lax.axis_index("seq")
     row_count = partial.shape[0] // count
@@ -416,6 +414,8 @@
         if k:
             held = lax.optimization_barrier((arrived[k], *sums[-2:]))
             arrived[k], sums[-2:] = held[0], held[1:]
+        if later and k == len(order) // 2:
+            arrived[k], *later = lax.optimization_barrier((arrived[k], *later))
         pair = block(n) + arrived[k].astype(wide)
         if k:
             sums[-1] = swapped(sums[-1], "seq", order[k - 1])
@@ -423,22 +423,15 @@
     total = sums[-1]
     for other in sums[:-1]:
         total = total + other.astype(wide)
-    return total
+    return (total, *later) if later else total
 
 
 def gather_dp(array):
-    size, place = lax.axis_size("dp"), lax.axis_index("dp")
-    rows, bit = array.shape[0], size // 2
-    held = jnp.zeros((size * rows,) + array.shape[1:], array.dtype)
-    blocks, order = array, [0]
+    blocks, bit = {0: array}, lax.axis_size("dp") // 2
     while bit:
-        blocks = jnp.concatenate([blocks, swapped(blocks, "dp", bit)], 0)
-        order = order + [n ^ bit for n in order]
+        blocks.update({n ^ bit: swapped(block, "dp", bit) for n, block in list(blocks.items())})
         bit //= 2
-    for k, n in enumerate(order):
-        block = blocks[k * rows : (k + 1) * rows]
-        held = lax.dynamic_update_slice_in_dim(held, block, (place ^ n) * rows, 0)
-    return held
+    return [blocks[n] for n in range(len(blocks))]
 
 
 def gather_team(rows):
@@ -463,12 +456,12 @@
     return partial
 
 
-def sum_row_halves(array, axis, bit):
+def row_halves(array, axis, bit):
     mine = ((lax.axis_index(axis) & bit) != 0).astype(jnp.int32)
     half = array.shape[0] // 2
     other = lax.dynamic_slice_in_dim(array, (1 - mine) * half, half).astype(jnp.bfloat16)
     kept = lax.dynamic_slice_in_dim(array, mine * half, half)
-    return kept.astype(jnp.float32) + swapped(other, axis, bit).astype(jnp.float32)
+    return kept, swapped(other, axis, bit)
 
 
 def to_seq(array):
@@ -490,35 +483,179 @@
     log_ref[...] = top + jnp.log(total)
 
 
-def attend_back_kernel(
-    query_ref,
-    key_ref,
-    value_ref,
-    query_pos_ref,
-    key_pos_ref,
-    out_ref,
-    log_ref,
-    grad_ref,
-    grad_query_ref,
-    grad_key_ref,
-    grad_value_ref,
-):
-    @pl.when(pl.program_id(0) == 0)
-    def _():
-        grad_key_ref[...] = jnp.zeros_like(grad_key_ref)
-        grad_value_ref[...] = jnp.zeros_like(grad_value_ref)
-
-    scale = query_ref.shape[-1] ** (-0.5)
-    query, key, grad = query_ref[...], key_ref[...], grad_ref[...]
-    scores = contract_cols(query, key) * scale
-    allowed = key_pos_ref[...] <= query_pos_ref[...]
-    probs = jnp.where(allowed, jnp.exp(scores - log_ref[...]), 0.0)
-    delta = jnp.sum(grad.astype(jnp.float32) * out_ref[...], axis=-1, keepdims=True)
-    grad_probs = contract_cols(grad, value_ref[...])
-    grad_scores = (probs * (grad_probs - delta)).astype(jnp.bfloat16)
-    grad_value_ref[...] += contract_rows(probs.astype(jnp.bfloat16), grad)
-    grad_query_ref[...] = jnp.dot(grad_scores, key, preferred_element_type=jnp.float32) * scale
-    grad_key_ref[...] += contract_rows(grad_scores, query) * scale
+def rope_rows(values, cosine, sine):
+    return values * cosine + pltpu.roll(values, values.shape[-1] // 2, 1) * sine
+
+
+def rope_rows_back(grad, cosine, sine):
+    return grad * cosine + pltpu.roll(grad * sine, grad.shape[-1] // 2, 1)
+
+
+def rms_back(grad, values, gain):
+    inverse = lax.rsqrt(jnp.mean(values * values, axis=-1, keepdims=True) + eps_model)
+    weighted = grad * gain
+    shared = inverse * inverse * jnp.mean(weighted * values, axis=-1, keepdims=True)
+    gain_grad = jnp.sum(grad * values * inverse, axis=0, keepdims=True)
+    return inverse * (weighted - values * shared), gain_grad
+
+
+def prepare_kernel(groups, parts, place_ref, tokens_ref, *refs):
+    weights = refs[:parts]
+    cosine_ref, sine_ref, head_gains_ref = refs[parts : parts + 3]
+    (matrix_ref, gains_ref, normed_ref, pre_ref, query_ref, key_ref, value_ref) = refs[parts + 3 :]
+    part_rows = weights[0].shape[0]
+    length, head_dim = tokens_ref.shape[0], head_gains_ref.shape[1]
+    qkv_cols = (groups + 2) * head_dim
+    for n in range(parts):
+        start = pl.multiple_of((place_ref[1] ^ n) * part_rows, part_rows)
+        matrix_ref[pl.ds(start, part_rows), :] = weights[n][...]
+    matrix_cols = matrix_ref.shape[1]
+    gains = matrix_ref[:, matrix_cols - 128 :].astype(jnp.float32).T[:8]
+    gains_ref[...] = gains
+    step = math.gcd(length, 256)
+    for start in range(0, length, step):
+        here = slice(start, start + step)
+        normed = rms_scale(tokens_ref[here, :].astype(jnp.float32), gains[:1])
+        normed_ref[here, :] = normed.astype(jnp.bfloat16)
+        pre = jnp.dot(
+            normed_ref[here, :], matrix_ref[:, :qkv_cols], preferred_element_type=jnp.float32
+        )
+        pre_ref[here, :] = pre[:, : qkv_cols - head_dim]
+        value_ref[here, :] = pre[:, qkv_cols - head_dim :].astype(jnp.bfloat16)
+        cosine, sine = cosine_ref[here, :], sine_ref[here, :]
+        for n in range(groups + 1):
+            gain = head_gains_ref[(0 if n < groups else 1), :][None]
+            head = rms_scale(pre[:, n * head_dim : (n + 1) * head_dim], gain)
+            head = rope_rows(head, cosine, sine).astype(jnp.bfloat16)
+            if n < groups:
+                query_ref[n * length + start : n * length + start + step, :] = head
+            else:
+                key_ref[here, :] = head
+
+
+def attend_back_kernel(groups, count, place_ref, *refs):
+    blocks = refs[:count]
+    (matrix_ref, query_ref, key_ref, value_ref, query_pos_ref, key_pos_ref, out_ref, log_ref) = refs[
+        count : count + 8
+    ]
+    (pre_ref, cosine_ref, sine_ref, head_gains_ref, tokens_ref, normed_ref) = refs[
+        count + 8 : count + 14
+    ]
+    (partial_ref, grads_ref, gain_ref, head_gain_ref) = refs[count + 14 : count + 18]
+    middle, grad_qkv, grad_key, grad_value = refs[count + 18 :]
+    low, wide = jnp.bfloat16, jnp.float32
+    row_count = blocks[0].shape[0]
+    length, head_dim = key_ref.shape
+    pair_cols = groups * head_dim
+    qkv_cols = pair_cols + 2 * head_dim
+    scale = head_dim ** (-0.5)
+    for n in range(count):
+        start = pl.multiple_of((place_ref[0] ^ n) * row_count, row_count)
+        middle[pl.ds(start, row_count), :] = blocks[n][...]
+    grad_key[...] = jnp.zeros_like(grad_key)
+    grad_value[...] = jnp.zeros_like(grad_value)
+    key, value = key_ref[...], value_ref[...]
+    query_gain, key_gain = head_gains_ref[0, :][None], head_gains_ref[1, :][None]
+    gain_query = jnp.zeros((1, head_dim), wide)
+    step = 2 * row_count
+    for start in range(0, length, step):
+        here = slice(start, start + step)
+        grad_att = jnp.dot(
+            middle[here, :],
+            matrix_ref[:, qkv_cols : qkv_cols + pair_cols],
+            preferred_element_type=wide,
+        ).astype(low)
+        allowed = key_pos_ref[...] <= query_pos_ref[here, :]
+        for n in range(groups):
+            there = slice(n * length + start, n * length + start + step)
+            cols = slice(n * head_dim, (n + 1) * head_dim)
+            query, grad = query_ref[there, :], grad_att[:, cols]
+            scores = contract_cols(query, key) * scale
+            probs = jnp.where(allowed, jnp.exp(scores - log_ref[there, :]), 0.0)
+            delta = jnp.sum(grad.astype(wide) * out_ref[there, :], axis=-1, keepdims=True)
+            grad_scores = (probs * (contract_cols(grad, value) - delta)).astype(low)
+            grad_value[...] += contract_rows(probs.astype(low), grad)
+            grad_key[...] += contract_rows(grad_scores, query) * scale
+            turned = jnp.dot(grad_scores, key, preferred_element_type=wide) * scale
+            turned = rope_rows_back(turned, cosine_ref[here, :], sine_ref[here, :])
+            before, gain = rms_back(turned, pre_ref[here, cols], query_gain)
+            grad_qkv[here, cols] = before.astype(low)
+            gain_query = gain_query + gain
+    turned = rope_rows_back(grad_key[...], cosine_ref[...], sine_ref[...])
+    before, gain_key = rms_back(turned, pre_ref[:, pair_cols : pair_cols + head_dim], key_gain)
+    grad_qkv[:, pair_cols : pair_cols + head_dim] = before.astype(low)
+    grad_qkv[:, pair_cols + head_dim :] = grad_value[...].astype(low)
+    head_gain_ref[0:1, :] = gain_query
+    head_gain_ref[1:2, :] = gain_key
+    gain_one = jnp.zeros((1, tokens_ref.shape[1]), wide)
+    for start in range(0, length, step):
+        here = slice(start, start + step)
+        partial = contract_cols(grad_qkv[here, :], matrix_ref[:, :qkv_cols])
+        partial_ref[here, :] = partial
+        rows = tokens_ref[here, :].astype(wide)
+        inverse = lax.rsqrt(jnp.mean(rows * rows, axis=-1, keepdims=True) + eps_model)
+        gain_one = gain_one + jnp.sum(partial * (rows * inverse), axis=0, keepdims=True)
+    gain_ref[0:1, :] = gain_one
+    grads_ref[:, :qkv_cols] = contract_rows(normed_ref[...], grad_qkv[...]).astype(low)
+    for n in range(groups):
+        attended = out_ref[n * length : (n + 1) * length, :].astype(low)
+        cols = slice(qkv_cols + n * head_dim, qkv_cols + (n + 1) * head_dim)
+        grads_ref[:, cols] = contract_rows(middle[...], attended).astype(low)
+
+
+def whole_specs(arrays):
+    return [pl.BlockSpec(memory_space=pltpu.VMEM) for _ in arrays]
+
+
+def prepare(place, rows, weights, cosine, sine, head_gains, groups):
+    low, wide = jnp.bfloat16, jnp.float32
+    length, width = rows.shape
+    head_dim = head_gains.shape[1]
+    matrix_rows, matrix_cols = len(weights) * weights[0].shape[0], weights[0].shape[1]
+    operands = (rows, *weights, cosine, sine, head_gains)
+    outs = [
+        ((matrix_rows, matrix_cols), low),
+        ((8, width), wide),
+        ((length, width), low),
+        ((length, (groups + 1) * head_dim), wide),
+        ((groups * length, head_dim), low),
+        ((length, head_dim), low),
+        ((length, head_dim), low),
+    ]
+    return pl.pallas_call(
+        functools.partial(prepare_kernel, groups, len(weights)),
+        in_specs=[pl.BlockSpec(memory_space=pltpu.SMEM)] + whole_specs(operands),
+        out_specs=whole_specs(outs),
+        out_shape=[jax.ShapeDtypeStruct(*out) for out in outs],
+        compiler_params=pltpu.CompilerParams(vmem_limit_bytes=48 * 1024 * 1024),
+    )(place, *operands)
+
+
+def attend_back(place, blocks, operands, groups):
+    low, wide = jnp.bfloat16, jnp.float32
+    row_count, width = blocks[0].shape
+    length, head_dim = operands[2].shape
+    qkv_cols = (groups + 2) * head_dim
+    operands = (*blocks, *operands)
+    outs = [
+        ((length, width), wide),
+        ((width, qkv_cols + groups * head_dim), low),
+        ((8, width), wide),
+        ((8, head_dim), wide),
+    ]
+    return pl.pallas_call(
+        functools.partial(attend_back_kernel, groups, len(blocks)),
+        in_specs=[pl.BlockSpec(memory_space=pltpu.SMEM)] + whole_specs(operands),
+        out_specs=whole_specs(outs),
+        out_shape=[jax.ShapeDtypeStruct(*out) for out in outs],
+        scratch_shapes=[
+            pltpu.VMEM((length, width), low),
+            pltpu.VMEM((length, qkv_cols), low),
+            pltpu.VMEM((length, head_dim), wide),
+            pltpu.VMEM((length, head_dim), wide),
+        ],
+        compiler_params=pltpu.CompilerParams(vmem_limit_bytes=56 * 1024 * 1024),
+    )(place, *operands)
 
 
 def attend_specs(rows, length, head_dim, block):
@@ -554,31 +691,6 @@
         cost_estimate=attend_cost(rows, length, head_dim, 2),
         compiler_params=pltpu.CompilerParams(vmem_limit_bytes=40 * 1024 * 1024),
     )(query, key, value, query_pos, key_pos)
-
-
-def attend_back(query, key, value, query_pos, key_pos, attended, log_total, grad):
-    rows, head_dim = query.shape
-    length = key.shape[0]
-    grid, by_rows, by_row, whole, keys = attend_specs(rows, length, head_dim, 512)
-    return pl.pallas_call(
-        attend_back_kernel,
-        grid=grid,
-        in_specs=[by_rows, whole, whole, by_row, keys, by_rows, by_row, by_rows],
-        out_specs=[by_rows, whole, whole],
-        out_shape=[
-            jax.ShapeDtypeStruct((rows, head_dim), jnp.float32),
-            jax.ShapeDtypeStruct((length, head_dim), jnp.float32),
-            jax.ShapeDtypeStruct((length, head_dim), jnp.float32),
-        ],
-        cost_estimate=attend_cost(rows, length, head_dim, 5),
-        compiler_params=pltpu.CompilerParams(vmem_limit_bytes=48 * 1024 * 1024),
-    )(query, key, value, query_pos, key_pos, attended, log_total, grad)
-
-
-def rotate_rows(values, cosine, sine):
-    half_dim = values.shape[-1] // 2
-    turned = jnp.concatenate([-values[:, half_dim:], values[:, :half_dim]], -1)
-    return values * cosine + turned * sine
 
 
 def split_shards(
@@ -608,20 +720,22 @@
     span_len = row_count // 2
     seq_index = lax.axis_index("seq")
 
+    def cut(weight, parts):
+        return weight.reshape(weight_rows, parts, -1).transpose(1, 0, 2)
+
     seq_tokens = gathered(tokens, "seq")
     cotangent, tokens = lax.optimization_barrier((cotangent, tokens))
-
-    def cut(weight, parts):
-        return weight.reshape(weight_rows, parts, -1).transpose(1, 0, 2)
 
     gain_cols = jnp.pad(norm_gains.T, ((0, 0), (0, 126)))
     gain_cols = jnp.broadcast_to(gain_cols[None], (seq_size, weight_rows, 128))
     first_part = [cut(w, seq_size) for w in (w_query, key_matrix, value_matrix, w_output.T)]
-    first_part = to_seq(jnp.concatenate(first_part + [gain_cols], -1))
+    first_part = jnp.concatenate(first_part + [gain_cols], -1)
+    first_part = to_seq(first_part)
     first_part = first_part.reshape(seq_size * weight_rows, -1)
     first_part = gather_dp(first_part)
-    team_cotangent = gather_team(cotangent)
-    first_part, w_gate, w_up, w_down = lax.optimization_barrier((first_part, w_gate, w_up, w_down))
+    *first_part, w_gate, w_up, w_down = lax.optimization_barrier(
+        (*first_part, w_gate, w_up, w_down)
+    )
     second_part = jnp.concatenate([cut(w, dp_size) for w in (w_gate, w_up, w_down.T)], -1)
     second_part = over_dp(second_part).reshape(dp_size * weight_rows, -1)
     seq_tokens, second_part = lax.optimization_barrier((seq_tokens, second_part))
@@ -629,38 +743,18 @@
     second_part = second_part.transpose(1, 0, 2, 3).reshape(width, -1)
     w_gate_up = second_part[:, : 2 * unit_cols]
     wd_turned = second_part[:, 2 * unit_cols :]
-    w_qkv = first_part[:, :qkv_cols]
-    wo_turned = first_part[:, qkv_cols : qkv_cols + pair_cols]
-    gains = first_part[:, qkv_cols + pair_cols :][:, :2].T.astype(wide)
     offsets = jnp.arange(span_len, dtype=jnp.int32)
     positions = (span_order[0][:, None] * span_len + offsets).reshape(length)
     cosine, sine = rope_tables(positions, head_dim)
+    half_dim = head_dim // 2
+    sine = jnp.concatenate([-sine[:, :half_dim], sine[:, half_dim:]], 1)
     gains_head = head_gains.astype(wide)
     inputs = tokens.astype(wide)
-    seq_inputs = seq_tokens.astype(wide)
-    inverse = lax.rsqrt(jnp.mean(seq_inputs * seq_inputs, axis=-1, keepdims=True) + eps_model)
-    seq_scaled = seq_inputs * inverse
-    normed_low = (seq_scaled * gains[0]).astype(low)
-    qkv_pre = jnp.dot(normed_low, w_qkv, preferred_element_type=wide)
-
-    def prepare(flat, gain):
-        return rotate_rows(rms_scale(flat, gain), cosine, sine)
-
-    def head_of(array, n):
-        return array[:, n * head_dim : (n + 1) * head_dim]
-
-    query_rot, query_back = [], []
-    for n in range(groups):
-        rotated, back = jax.vjp(prepare, head_of(qkv_pre, n), gains_head[0])
-        query_rot.append(rotated.astype(low))
-        query_back.append(back)
-    key_rot, key_back = jax.vjp(prepare, head_of(qkv_pre, groups), gains_head[1])
-    key_low = key_rot.astype(low)
-    value_low = head_of(qkv_pre, groups + 1).astype(low)
-    query_low = jnp.concatenate(query_rot, 0)
-
-    def heads_down(array):
-        return jnp.concatenate([head_of(array, n) for n in range(groups)], 0)
+    place = jnp.stack([seq_index, lax.axis_index("dp")]).astype(jnp.int32)
+    matrix, gains, normed_low, qkv_pre, query_low, key_low, value_low = prepare(
+        place, seq_tokens, first_part, cosine, sine, gains_head, groups
+    )
+    wo_turned = matrix[:, qkv_cols : qkv_cols + pair_cols]
 
     def heads_across(array):
         return jnp.concatenate([array[n * length : (n + 1) * length] for n in range(groups)], 1)
@@ -668,9 +762,9 @@
     query_pos = jnp.concatenate([positions] * groups)[:, None]
     key_pos = positions[None, :]
     attended, attended_low, log_total = attend(query_low, key_low, value_low, query_pos, key_pos)
-    attended_low = heads_across(attended_low)
-    middle = inputs + scatter_seq(contract_cols(attended_low, wo_turned))
-
+    middle = inputs + scatter_seq(contract_cols(heads_across(attended_low), wo_turned))
+
+    team_cotangent = gather_team(cotangent)
     normed_two, norm_two_back = jax.vjp(rms_scale, middle, gains[1])
     normed_two_low = gather_team(normed_two.astype(low))
     gate_up = jnp.dot(normed_two_low, w_gate_up, preferred_element_type=wide)
@@ -695,59 +789,36 @@
     grad_middle = cotangent.astype(wide) + grad_middle_norm
     middle_low = gather_seq(grad_middle.astype(low))
     out_partial = contract_cols(hidden_low, wd_turned)
-    out_partial, middle_low = lax.optimization_barrier((out_partial, middle_low))
+    out_partial, *middle_low = lax.optimization_barrier((out_partial, *middle_low))
     out_partial = scatter_step(out_partial, 1)
 
-    grad_att = jnp.dot(middle_low, wo_turned, preferred_element_type=wide).astype(low)
-    grad_att, out_partial = lax.optimization_barrier((grad_att, out_partial))
+    middle_low[0], out_partial = lax.optimization_barrier((middle_low[0], out_partial))
     output = middle + scatter_rest(out_partial)
-    grad_query, grad_key, grad_value = attend_back(
-        query_low,
-        key_low,
-        value_low,
-        query_pos,
-        key_pos,
-        attended,
-        log_total,
-        heads_down(grad_att),
-    )
-    grad_query, grad_key, grad_value, output = lax.optimization_barrier(
-        (grad_query, grad_key, grad_value, output)
-    )
-    grad_qkv, gain_query = [], 0.0
-    for n in range(groups):
-        before, gain = query_back[n](grad_query[n * length : (n + 1) * length])
-        grad_qkv.append(before.astype(low))
-        gain_query = gain_query + gain
-    before, gain_key = key_back(grad_key)
-    grad_qkv = jnp.concatenate(grad_qkv + [before.astype(low), grad_value.astype(low)], -1)
-    partial = contract_cols(grad_qkv, w_qkv)
-    grad_gain_one = jnp.sum(partial * seq_scaled, axis=0)
+    operands = (matrix, query_low, key_low, value_low, query_pos, key_pos, attended, log_total)
+    operands = operands + (qkv_pre, cosine, sine, gains_head, seq_tokens, normed_low)
+    partial, first_grads, grad_gain_one, head_gain = attend_back(place, middle_low, operands, groups)
+    partial, first_grads, output = lax.optimization_barrier((partial, first_grads, output))
+    _, norm_back = jax.vjp(lambda values: rms_scale(values, gains[0]), inputs)
     def in_columns(cols):
         return jnp.pad(cols, ((0, 0), (0, 128 - cols.shape[1])))
 
     seq_rows = seq_size * weight_rows
-    head_gain = jnp.stack([gain_query, gain_key], 1)
+    head_gain = head_gain[:2].T
     head_gain = jnp.pad(head_gain, ((0, seq_rows - head_dim), (0, 0)))
     head_gain = jnp.concatenate([head_gain] * dp_size, 0)
-    gain_cols = jnp.concatenate([jnp.stack([grad_gain_one, grad_gain_two], 1), head_gain], 1)
-    first_grads = jnp.concatenate(
-        [
-            contract_rows(normed_low, grad_qkv).astype(low),
-            contract_rows(middle_low, attended_low).astype(low),
-            in_columns(gain_cols).astype(low),
-        ],
-        1,
-    )
+    gain_cols = jnp.concatenate([jnp.stack([grad_gain_one[0], grad_gain_two], 1), head_gain], 1)
+    first_grads = jnp.concatenate([first_grads, in_columns(gain_cols).astype(low)], 1)
     first_grads, partial = lax.optimization_barrier((first_grads, partial))
-    bit = dp_size // 2
+    first_grads, other = row_halves(first_grads, "dp", dp_size // 2)
+    grad_normed, other, second_grads = scatter_seq(partial, (other, second_grads))
+    first_grads = first_grads.astype(wide) + other.astype(wide)
+    bit = dp_size // 4
     while bit:
-        first_grads = sum_row_halves(first_grads, "dp", bit)
+        first_grads, other = row_halves(first_grads, "dp", bit)
+        first_grads = first_grads.astype(wide) + other.astype(wide)
         bit //= 2
-    grad_normed = scatter_seq(partial)
-    grad_normed, first_grads, second_grads = lax.optimization_barrier(
-        (grad_normed, first_grads.astype(low), second_grads)
-    )
+    first_grads = first_grads.astype(low)
+    second_grads = over_dp(second_grads.reshape(dp_size, weight_rows, -1))
     _, norm_back = jax.vjp(lambda values: rms_scale(values, gains[0]), inputs)
     grad_input = grad_middle + norm_back(grad_normed)[0]
 
@@ -758,12 +829,11 @@
     head_gain = jnp.concatenate([head_gain] * seq_size, 0)
     gain_cols = in_columns(jnp.concatenate([gain_cols[:, :2], head_gain], 1))
     first_grads = jnp.concatenate([first_grads[:, :matrix_cols], gain_cols], 1)
+    first_grads, second_grads = lax.optimization_barrier((first_grads, second_grads))
     first_grads = to_seq(first_grads.reshape(seq_size, weight_rows, -1))
     gain_cols = jnp.sum(first_grads[..., matrix_cols:].astype(wide), 0)
     grad_norm = gain_cols[:, :2].T
     grad_head = gain_cols[:, 2 : 2 + head_width].reshape(head_dim, 2).T
-
-    second_grads = over_dp(second_grads.reshape(dp_size, weight_rows, -1))
 
     def joined(blocks, start, cols):
         parts = [blocks[n, :, start : start + cols] for n in range(blocks.shape[0])]

time: 406 us -> 382 us (0.941); the launches traced: 405 us -> 376 us
  starting transfers between devices: 82.7 us -> 54.8 us
  other arithmetic: 41 us -> 22.9 us
  Pallas kernels: 15.6 us -> 32.2 us
  blocking collectives: 28.6 us -> 41.2 us
  local copies, waits for them, and re-layouts: 36.4 us -> 24.5 us
  matrix products: 18.5 us -> 14 us
    ppermute x33 -> x34, starting transfers between devices: 69.4 us -> 47.8 us  [swapped(): lax.ppermute(array, axis, [(i, i ^ by) for i in range(lax.axis_size(axis))])]
    ppermute x33 -> x34, waiting for transfers between devices: 138 us -> 158 us  [swapped(): lax.ppermute(array, axis, [(i, i ^ by) for i in range(lax.axis_size(axis))])]
    all_to_all x2 -> x1, waiting for transfers between devices: 17.9 us -> 0.01 us  [over_dp(): return lax.all_to_all(array, 'dp', 0, 0, tiled=True)]
    pallas_call x1 -> x2, Pallas kernels: 8.58 us -> 25.2 us  [the longest x1 19.5 us: attend_back(): pl.pallas_call(functools.partial(attend_back_kernel, groups, len(blocks))...]
    all_to_all x0 -> x1, blocking collectives: none -> 12.6 us  [over_dp(): return lax.all_to_all(array, 'dp', 0, 0, tiled=True)]
    unnamed x117 -> x121, local copies, waits for them, and re-layouts: 17.7 us -> 11.9 us
  transfers between devices with their start and end apart: 39 -> 39, of which waited for: 23 -> 24; matrix products, arithmetic and copies ran while one was open for 17% -> 11% of each run, Pallas kernels for 4% -> 9%
where the time goes in v3:
time: 382 us; the launch traced here: 376 us
  waiting for transfers between devices  171 us (45%)
  starting transfers between devices  54.8 us (14%)
  blocking collectives  41.2 us (11%)
  Pallas kernels  32.2 us (8%)
  local copies, waits for them, and re-layouts  24.5 us (6%)
  other arithmetic  22.9 us (6%)
  between operations  15.3 us (4%)
  matrix products  14 us (4%)
    ppermute x34, waiting for transfers between devices, swapped(): lax.ppermute(array, axis, [(i, i ^ by) for i in range(lax.axis_size(axis))])  158 us
    ppermute x34, starting transfers between devices, swapped(): lax.ppermute(array, axis, [(i, i ^ by) for i in range(lax.axis_size(axis))])  47.8 us
    all_to_all x1, blocking collectives, to_seq(): return lax.all_to_all(array, 'seq', 0, 0, tiled=True)  28.6 us
    pallas_call x1, Pallas kernels, attend_back(): pl.pallas_call(functools.partial(attend_back_kernel, groups, len(blocks))...  19.5 us
    all_to_all x1, blocking collectives, over_dp(): return lax.all_to_all(array, 'dp', 0, 0, tiled=True)  12.6 us
    unnamed x121, local copies, waits for them, and re-layouts  11.9 us
    all_to_all x1, waiting for transfers between devices, to_seq(): return lax.all_to_all(array, 'seq', 0, 0, tiled=True)  8.68 us
    dot_general x3, matrix products, contract_cols(): lax.dot_general(left, right, (((1,), (1,)), ((), ())), preferred_element_...  7.77 us
  transfers between devices with their start and end apart: 39, of which 24 were waited for; matrix products, arithmetic and copies ran while one was open for 11% of the time, Pallas kernels for 9%

profile of v3, /device:TPU:0, one launch (start us, length us, event | category | flops | bytes accessed | tf_op | source)
XLA Modules:
  0.0 375.6 jit_solution(16972380624674046522)
XLA Ops:
  11.5 28.6 %all_to_all.20 = bf16[8,32,896]{2,1,0:T(8,128)(2,1)S(1)} all-to-all(bf16[8,32,896]{2,1,0:T(8,128)(2,1)S(1)} %constant_dynamic-update-slice_fusion), channel_id=1, replica_groups=mesh['dp'=4,'seq'=8] {'seq'}, dimensions={0} | all-to-all | bytes 917504 | tf_op jit(solution)/shard_map/all_to_all | solution.py:468
  41.7 7.0 %collective-permute-done.1.refs_2_ = bf16[256,896]{1,0:T(8,128)(2,1)S(1)} collective-permute-done((bf16[256,896]{1,0:T(8,128)(2,1)S(1)}, bf16[256,896]{1,0:T(8,128)(2,1)S(1)}, u32[]{:S(2)}, u32[]{:S(2)}) %collective-permute-start.1) | collective-permute-done | bytes 458784 | tf_op jit(solution)/shard_map/ppermute | solution.py:376
  52.0 12.6 %all_to_all.21 = bf16[4,32,2304]{2,1,0:T(8,128)(2,1)} all-to-all(bf16[4,32,2304]{2,1,0:T(8,128)(2,1)S(1)} %copy.108), channel_id=1, replica_groups=mesh['dp'=4,'seq'=8] {'dp'}, dimensions={0} | all-to-all | bytes 1179648 | tf_op jit(solution)/shard_map/all_to_all | solution.py:380
  70.7 5.7 %shard_map.203 = (bf16[1024,896]{1,0:T(8,128)(2,1)}, f32[8,1024]{1,0:T(8,128)S(1)}, bf16[1024,1024]{1,0:T(8,128)(2,1)}, f32[1024,384]{1,0:T(8,128)S(1)}, bf16[20...) custom-call(s32[2]{0:T(128)S(1)} %pad_add_fusion.1.place_ref, ...), custom_call_target="tpu_custom_call" | custom-call | tf_op jit(solution)/shard_map/pallas_call | solution.py:625
  76.5 7.0 %shard_map.204 = (f32[2048,128]{1,0:T(8,128)S(1)}, bf16[2048,128]{1,0:T(8,128)(2,1)S(1)}, f32[2048,1]{1,0:T(8,128)S(1)}) custom-call(bf16[2048,128]{1,0:T(8,128)(2,1)S(1)} %get-tuple-element.87.query_ref.refs_9_, bf16[1024,128]{1,0:T(8,128)(2,1)S(1)} %get-tuple-element.88.key_ref.refs_10_, bf16[1024,128]{1,0:T(8,128)(2,1)S(1)} %get-tuple-element.89.value_ref.refs_11_, ...), custom_call_target="tpu_custom_call" | custom-call | flops 1073741824 | bytes 4194304 | tf_op jit(solution)/shard_map/pallas_call | solution.py:681
  90.5 6.7 %collective-permute-done.6 = bf16[128,1024]{1,0:T(8,128)(2,1)S(1)} collective-permute-done((bf16[128,1024]{1,0:T(8,128)(2,1)S(1)}, bf16[128,1024]{1,0:T(8,128)(2,1)S(1)}, u32[]{:S(2)}, u32[]{:S(2)}) %collective-permute-start.6) | collective-permute-done | bytes 262176 | tf_op jit(solution)/shard_map/ppermute | solution.py:376
  98.2 4.5 %collective-permute-done.5 = bf16[128,1024]{1,0:T(8,128)(2,1)S(1)} collective-permute-done((bf16[128,1024]{1,0:T(8,128)(2,1)S(1)}, bf16[128,1024]{1,0:T(8,128)(2,1)S(1)}, u32[]{:S(2)}, u32[]{:S(2)}) %collective-permute-start.5) | collective-permute-done | bytes 262176 | tf_op jit(solution)/shard_map/ppermute | solution.py:376
  108.9 7.6 %collective-permute-done.7 = bf16[128,1024]{1,0:T(8,128)(2,1)S(1)} collective-permute-done((bf16[128,1024]{1,0:T(8,128)(2,1)S(1)}, bf16[128,1024]{1,0:T(8,128)(2,1)S(1)}, u32[]{:S(2)}, u32[]{:S(2)}) %collective-permute-start.7) | collective-permute-done | bytes 262176 | tf_op jit(solution)/shard_map/ppermute | solution.py:376
  116.4 21.7 %collective-permute-start.8 = (bf16[128,1024]{1,0:T(8,128)(2,1)S(1)}, bf16[128,1024]{1,0:T(8,128)(2,1)S(1)}, u32[]{:S(2)}, u32[]{:S(2)}) collective-permute-start(bf16[128,1024]{1,0:T(8,128)(2,1)S(1)} %add_convert_fusion.5), channel_id=1, source_target_pairs={{0,4},{1,5},{2,6},{3,7},{4,0},{5,1},{6,2},{7,3},{8,12},{9,13},{10,... | collective-permute-start | bytes 786440 | tf_op jit(solution)/shard_map/ppermute | solution.py:376
  139.2 14.5 %collective-permute-done.8 = bf16[128,1024]{1,0:T(8,128)(2,1)S(1)} collective-permute-done((bf16[128,1024]{1,0:T(8,128)(2,1)S(1)}, bf16[128,1024]{1,0:T(8,128)(2,1)S(1)}, u32[]{:S(2)}, u32[]{:S(2)}) %collective-permute-start.8) | collective-permute-done | bytes 262176 | tf_op jit(solution)/shard_map/ppermute | solution.py:376
  156.0 10.9 %collective-permute-done.9 = bf16[128,1024]{1,0:T(8,128)(2,1)S(1)} collective-permute-done((bf16[128,1024]{1,0:T(8,128)(2,1)S(1)}, bf16[128,1024]{1,0:T(8,128)(2,1)S(1)}, u32[]{:S(2)}, u32[]{:S(2)}) %collective-permute-start.9) | collective-permute-done | bytes 262176 | tf_op jit(solution)/shard_map/ppermute | solution.py:376
  170.1 5.8 %collective-permute-done.10 = bf16[128,1024]{1,0:T(8,128)(2,1)S(1)} collective-permute-done((bf16[128,1024]{1,0:T(8,128)(2,1)S(1)}, bf16[128,1024]{1,0:T(8,128)(2,1)S(1)}, u32[]{:S(2)}, u32[]{:S(2)}) %collective-permute-start.10) | collective-permute-done | bytes 262176 | tf_op jit(solution)/shard_map/ppermute | solution.py:376
  195.0 7.2 %collective-permute-done.15 = bf16[128,1024]{1,0:T(8,128)(2,1)S(1)} collective-permute-done((bf16[128,1024]{1,0:T(8,128)(2,1)S(1)}, bf16[128,1024]{1,0:T(8,128)(2,1)S(1)}, u32[]{:S(2)}, u32[]{:S(2)}) %collective-permute-start.15) | collective-permute-done | bytes 262176 | tf_op jit(solution)/shard_map/ppermute | solution.py:376
  207.2 11.9 %collective-permute-done.21.refs_6_ = bf16[128,1024]{1,0:T(8,128)(2,1)S(1)} collective-permute-done((bf16[128,1024]{1,0:T(8,128)(2,1)S(1)}, bf16[128,1024]{1,0:T(8,128)(2,1)S(1)}, u32[]{:S(2)}, u32[]{:S(2)}) %collective-permute-start.21) | collective-permute-done | bytes 262176 | tf_op jit(solution)/shard_map/ppermute | solution.py:376
  219.0 32.9 %collective-permute-done.19.refs_4_ = bf16[128,1024]{1,0:T(8,128)(2,1)S(1)} collective-permute-done((bf16[128,1024]{1,0:T(8,128)(2,1)S(1)}, bf16[128,1024]{1,0:T(8,128)(2,1)S(1)}, u32[]{:S(2)}, u32[]{:S(2)}) %collective-permute-start.19) | collective-permute-done | bytes 262176 | tf_op jit(solution)/shard_map/ppermute | solution.py:376
  257.8 4.7 %collective-permute-done.20.refs_5_ = bf16[128,1024]{1,0:T(8,128)(2,1)S(1)} collective-permute-done((bf16[128,1024]{1,0:T(8,128)(2,1)S(1)}, bf16[128,1024]{1,0:T(8,128)(2,1)S(1)}, u32[]{:S(2)}, u32[]{:S(2)}) %collective-permute-start.20) | collective-permute-done | bytes 262176 | tf_op jit(solution)/shard_map/ppermute | solution.py:376
  262.5 8.4 %collective-permute-done.18.refs_3_ = bf16[128,1024]{1,0:T(8,128)(2,1)S(1)} collective-permute-done((bf16[128,1024]{1,0:T(8,128)(2,1)S(1)}, bf16[128,1024]{1,0:T(8,128)(2,1)S(1)}, u32[]{:S(2)}, u32[]{:S(2)}) %collective-permute-start.18) | collective-permute-done | bytes 262176 | tf_op jit(solution)/shard_map/ppermute | solution.py:376
  277.5 19.5 %shard_map.205 = (f32[1024,1024]{1,0:T(8,128)}, bf16[1024,768]{1,0:T(8,128)(2,1)}, f32[8,1024]{1,0:T(8,128)}, f32[8,128]{1,0:T(8,128)}) custom-call(s32[2]{0:T(128)} %copy-done.17, bf16[128,1024]{1,0:T(8,128)(2,1)} %copy-done.25, bf16[128,1024]{1,0:T(8,128)(2,1)} %copy-done.31, bf16[128,1024]{1,0:T(8,128)(2,1)} %copy-done.30, bf16[128,1024]{1,0:T(8,128)(2,1)} %copy-done.34, ...), custom_call_target="tpu_custom_call" | custom-call | tf_op jit(solution)/shard_map/pallas_call | solution.py:646
  305.7 7.1 %collective-permute-done.28 = bf16[128,1024]{1,0:T(8,128)(2,1)S(1)} collective-permute-done((bf16[128,1024]{1,0:T(8,128)(2,1)S(1)}, bf16[128,1024]{1,0:T(8,128)(2,1)S(1)}, u32[]{:S(2)}, u32[]{:S(2)}) %collective-permute-start.28) | collective-permute-done | bytes 262176 | tf_op jit(solution)/shard_map/ppermute | solution.py:376
  312.9 5.5 %collective-permute-done.27 = bf16[128,1024]{1,0:T(8,128)(2,1)S(1)} collective-permute-done((bf16[128,1024]{1,0:T(8,128)(2,1)S(1)}, bf16[128,1024]{1,0:T(8,128)(2,1)S(1)}, u32[]{:S(2)}, u32[]{:S(2)}) %collective-permute-start.27) | collective-permute-done | bytes 262176 | tf_op jit(solution)/shard_map/ppermute | solution.py:376
  319.3 4.8 %collective-permute-done.26 = bf16[128,1024]{1,0:T(8,128)(2,1)S(1)} collective-permute-done((bf16[128,1024]{1,0:T(8,128)(2,1)S(1)}, bf16[128,1024]{1,0:T(8,128)(2,1)S(1)}, u32[]{:S(2)}, u32[]{:S(2)}) %collective-permute-start.26) | collective-permute-done | bytes 262176 | tf_op jit(solution)/shard_map/ppermute | solution.py:376
  324.1 4.1 %collective-permute-done.29 = bf16[128,1024]{1,0:T(8,128)(2,1)S(1)} collective-permute-done((bf16[128,1024]{1,0:T(8,128)(2,1)S(1)}, bf16[128,1024]{1,0:T(8,128)(2,1)S(1)}, u32[]{:S(2)}, u32[]{:S(2)}) %collective-permute-start.29) | collective-permute-done | bytes 262176 | tf_op jit(solution)/shard_map/ppermute | solution.py:376
  341.0 4.9 %collective-permute-done.32 = bf16[128,1024]{1,0:T(8,128)(2,1)S(1)} collective-permute-done((bf16[128,1024]{1,0:T(8,128)(2,1)S(1)}, bf16[128,1024]{1,0:T(8,128)(2,1)S(1)}, u32[]{:S(2)}, u32[]{:S(2)}) %collective-permute-start.32) | collective-permute-done | bytes 262176 | tf_op jit(solution)/shard_map/ppermute | solution.py:376
  355.5 8.7 %all-to-all-done.3 = bf16[8,32,896]{2,1,0:T(8,128)(2,1)S(1)} async-done(((bf16[8,32,896]{2,1,0:T(8,128)(2,1)}), bf16[8,32,896]{2,1,0:T(8,128)(2,1)S(1)}, u32[]{:S(2)}, u32[]{:S(2)}) %all-to-all-start.3) | async-done | bytes 458784 | tf_op jit(solution)/shard_map/all_to_all | solution.py:468
  (274 shorter events, 107.9 us)
Async XLA Ops:
  7.2 60.3 %all-gather.3.cloned.1.call-start = ((), (), s32[]{:S(2)}) async-start(), calls=%async_computation.5 | async-start | bytes 2359296 | tf_op jit(solution)/shard_map/all_gather | solution.py:384
  8.0 170.9 %all-gather.5.cloned.1.call-start = ((), (), s32[]{:S(2)}) async-start(), calls=%async_computation.6 | async-start | bytes 5308416 | tf_op jit(solution)/shard_map/all_gather | solution.py:384
  67.5 264.5 %reduce-scatter.2.cloned.1.call-start = ((), (), s32[]{:S(2)}) async-start(), calls=%async_computation.7 | async-start | bytes 5308416 | tf_op jit(solution)/shard_map/reduce_scatter | solution.py:388
  88.4 14.3 %collective-permute-start.5 = (bf16[128,1024]{1,0:T(8,128)(2,1)S(1)}, bf16[128,1024]{1,0:T(8,128)(2,1)S(1)}, u32[]{:S(2)}, u32[]{:S(2)}) collective-permute-start(bf16[128,1024]{1,0:T(8,128)(2,1)S(1)} %get-tuple-element.216), channel_id=1, source_target_pairs={{0,1},{1,0},{2,3},{3,2},{4,5},{5,4},{6,7},{7,6},{8,9},{9,8},{10,11... | collective-permute-start | bytes 786440 | tf_op jit(solution)/shard_map/ppermute | solution.py:376
  89.9 18.9 %collective-permute-start.4 = (bf16[128,1024]{1,0:T(8,128)(2,1)S(1)}, bf16[128,1024]{1,0:T(8,128)(2,1)S(1)}, u32[]{:S(2)}, u32[]{:S(2)}) collective-permute-start(bf16[128,1024]{1,0:T(8,128)(2,1)S(1)} %get-tuple-element.217), channel_id=1, source_target_pairs={{0,1},{1,0},{2,3},{3,2},{4,5},{5,4},{6,7},{7,6},{8,9},{9,8},{10,11... | collective-permute-start | bytes 786440 | tf_op jit(solution)/shard_map/ppermute | solution.py:376
  102.7 13.7 %collective-permute-start.7 = (bf16[128,1024]{1,0:T(8,128)(2,1)S(1)}, bf16[128,1024]{1,0:T(8,128)(2,1)S(1)}, u32[]{:S(2)}, u32[]{:S(2)}) collective-permute-start(bf16[128,1024]{1,0:T(8,128)(2,1)S(1)} %add_convert_fusion.6), channel_id=1, source_target_pairs={{0,6},{1,7},{2,4},{3,5},{4,2},{5,3},{6,0},{7,1},{8,14},{9,15},{10,... | collective-permute-start | bytes 786440 | tf_op jit(solution)/shard_map/ppermute | solution.py:376
  104.5 34.7 %collective-permute-start.3 = (bf16[128,1024]{1,0:T(8,128)(2,1)S(1)}, bf16[128,1024]{1,0:T(8,128)(2,1)S(1)}, u32[]{:S(2)}, u32[]{:S(2)}) collective-permute-start(bf16[128,1024]{1,0:T(8,128)(2,1)S(1)} %get-tuple-element.218), channel_id=1, source_target_pairs={{0,1},{1,0},{2,3},{3,2},{4,5},{5,4},{6,7},{7,6},{8,9},{9,8},{10,11... | collective-permute-start | bytes 786440 | tf_op jit(solution)/shard_map/ppermute | solution.py:376
  116.4 37.2 %collective-permute-start.8 = (bf16[128,1024]{1,0:T(8,128)(2,1)S(1)}, bf16[128,1024]{1,0:T(8,128)(2,1)S(1)}, u32[]{:S(2)}, u32[]{:S(2)}) collective-permute-start(bf16[128,1024]{1,0:T(8,128)(2,1)S(1)} %add_convert_fusion.5), channel_id=1, source_target_pairs={{0,4},{1,5},{2,6},{3,7},{4,0},{5,1},{6,2},{7,3},{8,12},{9,13},{10,... | collective-permute-start | bytes 786440 | tf_op jit(solution)/shard_map/ppermute | solution.py:376
  153.7 13.3 %collective-permute-start.9 = (bf16[128,1024]{1,0:T(8,128)(2,1)S(1)}, bf16[128,1024]{1,0:T(8,128)(2,1)S(1)}, u32[]{:S(2)}, u32[]{:S(2)}) collective-permute-start(bf16[128,1024]{1,0:T(8,128)(2,1)S(1)} %add_convert_fusion.4), channel_id=1, source_target_pairs={{0,2},{1,3},{2,0},{3,1},{4,6},{5,7},{6,4},{7,5},{8,10},{9,11},{10,... | collective-permute-start | bytes 786440 | tf_op jit(solution)/shard_map/ppermute | solution.py:376
  153.7 16.3 %collective-permute-start.12 = (bf16[128,1024]{1,0:T(8,128)(2,1)S(1)}, bf16[128,1024]{1,0:T(8,128)(2,1)S(1)}, u32[]{:S(2)}, u32[]{:S(2)}) collective-permute-start(bf16[128,1024]{1,0:T(8,128)(2,1)S(1)} %copy-done.23), channel_id=1, source_target_pairs={{0,16},{8,24},{16,0},{24,8},{1,17},{9,25},{17,1},{25,9},{2,18},{10... | collective-permute-start | bytes 786440 | tf_op jit(solution)/shard_map/ppermute | solution.py:376
  202.6 16.4 %collective-permute-start.21 = (bf16[128,1024]{1,0:T(8,128)(2,1)S(1)}, bf16[128,1024]{1,0:T(8,128)(2,1)S(1)}, u32[]{:S(2)}, u32[]{:S(2)}) collective-permute-start(bf16[128,1024]{1,0:T(8,128)(2,1)S(1)} %get-tuple-element.109.refs_0_), channel_id=1, source_target_pairs={{0,6},{1,7},{2,4},{3,5},{4,2},{5,3},{6,0},{7,1},{8,14},{9,15},{10,... | collective-permute-start | bytes 786440 | tf_op jit(solution)/shard_map/ppermute | solution.py:376
  203.2 48.7 %collective-permute-start.19 = (bf16[128,1024]{1,0:T(8,128)(2,1)S(1)}, bf16[128,1024]{1,0:T(8,128)(2,1)S(1)}, u32[]{:S(2)}, u32[]{:S(2)}) collective-permute-start(bf16[128,1024]{1,0:T(8,128)(2,1)S(1)} %get-tuple-element.109.refs_0_), channel_id=1, source_target_pairs={{0,4},{1,5},{2,6},{3,7},{4,0},{5,1},{6,2},{7,3},{8,12},{9,13},{10,... | collective-permute-start | bytes 786440 | tf_op jit(solution)/shard_map/ppermute | solution.py:376
  203.7 48.2 %collective-permute-start.17 = (bf16[128,1024]{1,0:T(8,128)(2,1)S(1)}, bf16[128,1024]{1,0:T(8,128)(2,1)S(1)}, u32[]{:S(2)}, u32[]{:S(2)}) collective-permute-start(bf16[128,1024]{1,0:T(8,128)(2,1)S(1)} %get-tuple-element.109.refs_0_), channel_id=1, source_target_pairs={{0,2},{1,3},{2,0},{3,1},{4,6},{5,7},{6,4},{7,5},{8,10},{9,11},{10,... | collective-permute-start | bytes 786440 | tf_op jit(solution)/shard_map/ppermute | solution.py:376
  207.1 50.7 %collective-permute-start.16 = (bf16[128,1024]{1,0:T(8,128)(2,1)S(1)}, bf16[128,1024]{1,0:T(8,128)(2,1)S(1)}, u32[]{:S(2)}, u32[]{:S(2)}) collective-permute-start(bf16[128,1024]{1,0:T(8,128)(2,1)S(1)} %get-tuple-element.109.refs_0_), channel_id=1, source_target_pairs={{0,1},{1,0},{2,3},{3,2},{4,5},{5,4},{6,7},{7,6},{8,9},{9,8},{10,11... | collective-permute-start | bytes 786440 | tf_op jit(solution)/shard_map/ppermute | solution.py:376
  219.0 38.7 %collective-permute-start.22 = (bf16[128,1024]{1,0:T(8,128)(2,1)S(1)}, bf16[128,1024]{1,0:T(8,128)(2,1)S(1)}, u32[]{:S(2)}, u32[]{:S(2)}) collective-permute-start(bf16[128,1024]{1,0:T(8,128)(2,1)S(1)} %collective-permute-done.21.refs_6_), channel_id=1, source_target_pairs={{0,1},{1,0},{2,3},{3,2},{4,5},{5,4},{6,7},{7,6},{8,9},{9,8},{10,11... | collective-permute-start | bytes 786440 | tf_op jit(solution)/shard_map/ppermute | solution.py:376
  251.9 19.0 %collective-permute-start.18 = (bf16[128,1024]{1,0:T(8,128)(2,1)S(1)}, bf16[128,1024]{1,0:T(8,128)(2,1)S(1)}, u32[]{:S(2)}, u32[]{:S(2)}) collective-permute-start(bf16[128,1024]{1,0:T(8,128)(2,1)S(1)} %collective-permute-done.17.refs_2_), channel_id=1, source_target_pairs={{0,1},{1,0},{2,3},{3,2},{4,5},{5,4},{6,7},{7,6},{8,9},{9,8},{10,11... | collective-permute-start | bytes 786440 | tf_op jit(solution)/shard_map/ppermute | solution.py:376
  276.3 22.4 %collective-permute-start.24 = (bf16[128,1024]{1,0:T(8,128)(2,1)S(1)}, bf16[128,1024]{1,0:T(8,128)(2,1)S(1)}, u32[]{:S(2)}, u32[]{:S(2)}) collective-permute-start(bf16[128,1024]{1,0:T(8,128)(2,1)S(1)} %slice.479), channel_id=1, source_target_pairs={{0,16},{8,24},{16,0},{24,8},{1,17},{9,25},{17,1},{25,9},{2,18},{10... | collective-permute-start | bytes 786440 | tf_op jit(solution)/shard_map/ppermute | solution.py:376
  301.4 30.6 %collective-permute-start.31 = (bf16[512,896]{1,0:T(8,128)(2,1)}, bf16[512,896]{1,0:T(8,128)(2,1)}, u32[]{:S(2)}, u32[]{:S(2)}) collective-permute-start(bf16[512,896]{1,0:T(8,128)(2,1)} %constant_dynamic-slice_fusion), channel_id=1, source_target_pairs={{0,16},{8,24},{16,0},{24,8},{1,17},{9,25},{17,1},{25,9},{2,18},{10... | collective-permute-start | bytes 2752520 | tf_op jit(solution)/shard_map/ppermute | solution.py:376
  303.7 14.8 %collective-permute-start.27 = (bf16[128,1024]{1,0:T(8,128)(2,1)S(1)}, bf16[128,1024]{1,0:T(8,128)(2,1)S(1)}, u32[]{:S(2)}, u32[]{:S(2)}) collective-permute-start(bf16[128,1024]{1,0:T(8,128)(2,1)S(1)} %get-tuple-element.212), channel_id=1, source_target_pairs={{0,1},{1,0},{2,3},{3,2},{4,5},{5,4},{6,7},{7,6},{8,9},{9,8},{10,11... | collective-permute-start | bytes 786440 | tf_op jit(solution)/shard_map/ppermute | solution.py:376
  305.7 18.4 %collective-permute-start.26 = (bf16[128,1024]{1,0:T(8,128)(2,1)S(1)}, bf16[128,1024]{1,0:T(8,128)(2,1)S(1)}, u32[]{:S(2)}, u32[]{:S(2)}) collective-permute-start(bf16[128,1024]{1,0:T(8,128)(2,1)S(1)} %get-tuple-element.213), channel_id=1, source_target_pairs={{0,1},{1,0},{2,3},{3,2},{4,5},{5,4},{6,7},{7,6},{8,9},{9,8},{10,11... | collective-permute-start | bytes 786440 | tf_op jit(solution)/shard_map/ppermute | solution.py:376
  318.5 18.2 %collective-permute-start.25 = (bf16[128,1024]{1,0:T(8,128)(2,1)}, bf16[128,1024]{1,0:T(8,128)(2,1)}, u32[]{:S(2)}, u32[]{:S(2)}) collective-permute-start(bf16[128,1024]{1,0:T(8,128)(2,1)} %get-tuple-element.214), channel_id=1, source_target_pairs={{0,1},{1,0},{2,3},{3,2},{4,5},{5,4},{6,7},{7,6},{8,9},{9,8},{10,11... | collective-permute-start | bytes 786440 | tf_op jit(solution)/shard_map/ppermute | solution.py:376
  328.2 11.3 %collective-permute-start.30 = (bf16[128,1024]{1,0:T(8,128)(2,1)}, bf16[128,1024]{1,0:T(8,128)(2,1)}, u32[]{:S(2)}, u32[]{:S(2)}) collective-permute-start(bf16[128,1024]{1,0:T(8,128)(2,1)} %add_convert_fusion.2), channel_id=1, source_target_pairs={{0,4},{1,5},{2,6},{3,7},{4,0},{5,1},{6,2},{7,3},{8,12},{9,13},{10,... | collective-permute-start | bytes 786440 | tf_op jit(solution)/shard_map/ppermute | solution.py:376
  332.0 17.6 %all-to-all-start.2 = ((bf16[4,32,2304]{2,1,0:T(8,128)(2,1)}), bf16[4,32,2304]{2,1,0:T(8,128)(2,1)S(1)}, u32[]{:S(2)}, u32[]{:S(2)}) async-start(bf16[4,32,2304]{2,1,0:T(8,128)(2,1)} %bitcast.250), calls=%async_computation.3 | async-start | bytes 1179648 | tf_op jit(solution)/shard_map/all_to_all | solution.py:380
  349.6 14.6 %all-to-all-start.3 = ((bf16[8,32,896]{2,1,0:T(8,128)(2,1)}), bf16[8,32,896]{2,1,0:T(8,128)(2,1)S(1)}, u32[]{:S(2)}, u32[]{:S(2)}) async-start(bf16[8,32,896]{2,1,0:T(8,128)(2,1)} %bitcast.29), calls=%async_computation.4 | async-start | bytes 917504 | tf_op jit(solution)/shard_map/all_to_all | solution.py:468
  (60 other events, 746.6 us)
Sparse Core Ops, SparseCore 0:
  10.2 57.2 all-gather.2
  69.7 94.7 all-gather.4
  193.6 118.8 reduce-scatter.1
